TPU v7x, 128 devices: a whole 4x4x4 slice. The times are simulated.
128 devices in a mesh: stn: 8 (over z, core), chan: 16 (over y, x).
Axes of the slice: x: 4, y: 4, z: 4, core: 2. Of those that a mesh axis runs over, the one named last changes fastest.
Arguments:
- voltages: bfloat16 [2, 1024, 256, 256], P(None, ('stn', 'chan')), may hold values from -6 to 6
- weights: bfloat16 [2, 256, 256, 1024], P(None, ('stn', 'chan')), may hold values from -0.125 to 0.125
- flags: int32 [128, 64], P(('stn', 'chan')), may hold values from 0 to 255
- dm_index: int32 [256], P(('stn', 'chan')), may hold values from 0 to 15
Outputs:
- dedispersed: bfloat16 [2, 256, 65536], P(None, ('stn', 'chan'))
- bandpass: float32 [256, 256], P(('stn', 'chan'))
Inputs may be any that keep to these rules, and one draw needn't show every extreme that they name: `flags`: each station group lists 64 channel numbers, repeats allowed.
All inputs are finite; a program needn't handle non-finite values.
Results may differ from a plain program's by a relative error of at most 0.0066.
Values may be sent and summed in bfloat16 or wider, within the bound.
A program may use at most 64 MiB of HBM per device.

v0:
```python
import math

import jax
import jax.numpy as jnp
from jax import lax
from jax.sharding import PartitionSpec as P

CHANNELS = 256
TAPS = 12
CHIRP = 1024
DMS = 16
GROUP = 8


def channel_mask(flag_rows, channel_ids):
    hit = jnp.any(flag_rows[:, :, None] == channel_ids[None, None, :], axis=1)
    return jnp.where(hit, 0.0, 1.0).astype(jnp.float32)


def dft_table(order):
    freqs = jnp.arange(CHANNELS, dtype=jnp.int32)
    phase = order[:, None] * freqs[None, :] % CHANNELS
    angle = 2.0 * math.pi / CHANNELS * phase.astype(jnp.float32)
    cosine = jnp.cos(angle) / math.sqrt(CHANNELS)
    sine = jnp.sin(angle) / math.sqrt(CHANNELS)
    upper = jnp.stack([cosine, sine], axis=1)
    lower = jnp.stack([-sine, cosine], axis=1)
    return jnp.stack([upper, lower], axis=0).astype(jnp.bfloat16)


def prototype():
    counter = jnp.arange(TAPS * CHANNELS, dtype=jnp.float32)
    offset = (counter + 0.5) / CHANNELS - TAPS / 2.0
    window = 0.54 + 0.46 * jnp.cos(math.pi * offset / (TAPS / 2.0))
    return (jnp.sinc(offset) * window).reshape(TAPS, CHANNELS)


def chirp_table(dm_value):
    nblock = CHIRP // CHANNELS + 1
    blocks = jnp.arange(nblock, dtype=jnp.int32)[:, None, None]
    inner = jnp.arange(CHANNELS, dtype=jnp.int32)[None, :, None]
    outer = jnp.arange(CHANNELS, dtype=jnp.int32)[None, None, :]
    lag = blocks * CHANNELS + inner - outer
    valid = (lag >= 0) & (lag < CHIRP)
    lagc = jnp.clip(lag, 0, CHIRP - 1)
    phase = (dm_value + 1) * lagc * lagc % (2 * DMS * CHIRP)
    angle = math.pi * phase.astype(jnp.float32) / (DMS * CHIRP)
    real_part = jnp.where(valid, jnp.cos(angle), 0.0) / math.sqrt(CHIRP)
    imag_part = jnp.where(valid, jnp.sin(angle), 0.0) / math.sqrt(CHIRP)
    from_real = jnp.stack([real_part, -imag_part], axis=2)
    from_imag = jnp.stack([imag_part, real_part], axis=2)
    return jnp.stack([from_real, from_imag], axis=1).astype(jnp.bfloat16)


def stack_weights(weights):
    real_row = jnp.concatenate([weights[0], -weights[1]], axis=-1)
    imag_row = jnp.concatenate([weights[1], weights[0]], axis=-1)
    return jnp.stack([real_row, imag_row], axis=1)


def beamform(stacked, gathered):
    joined = gathered.reshape(
        gathered.shape[0] * gathered.shape[1], gathered.shape[2], gathered.shape[3]
    )
    beams = jnp.einsum("cpbk,kct->pbct", stacked, joined, preferred_element_type=jnp.float32)
    return beams.astype(jnp.bfloat16)


def on_device(voltages, weights, flags, dm_index):
    time_len = voltages.shape[3]
    keep = jnp.repeat(channel_mask(flags, jnp.arange(CHANNELS, dtype=jnp.int32)), GROUP, axis=0)
    outgoing = voltages * keep[None, :, :, None].astype(jnp.bfloat16)
    stacked = stack_weights(weights)
    beams = beamform(
        stacked, lax.all_to_all(outgoing, ("stn", "chan"), split_axis=2, concat_axis=1, tiled=True)
    )
    received = lax.all_to_all(beams, ("stn", "chan"), split_axis=1, concat_axis=2, tiled=True)
    order = jnp.arange(CHANNELS, dtype=jnp.int32)
    values = received.astype(jnp.float32)
    bandpass = jnp.mean(values[0] * values[0] + values[1] * values[1], axis=2)
    spectra = jnp.einsum(
        "pbct,pcqk->qbtk", received, dft_table(order), preferred_element_type=jnp.float32
    )
    taps = prototype()
    padded = jnp.pad(spectra, ((0, 0), (0, 0), (TAPS - 1, 0), (0, 0)))
    series = jnp.zeros_like(spectra)
    for tap in range(TAPS):
        series = (
            series
            + taps[tap][None, None, None, :]
            * padded[:, :, TAPS - 1 - tap : TAPS - 1 - tap + time_len, :]
        )
    series = series.astype(jnp.bfloat16)
    nblock = CHIRP // CHANNELS + 1
    tables = jax.vmap(chirp_table)(dm_index)
    longer = jnp.pad(series, ((0, 0), (0, 0), (0, nblock - 1), (0, 0)))
    result = jnp.zeros(series.shape, jnp.float32)
    for blk in range(nblock):
        result = result + jnp.einsum(
            "pbtu,bpuqa->qbta",
            longer[:, :, blk : blk + time_len, :],
            tables[:, blk],
            preferred_element_type=jnp.float32,
        )
    dedispersed = result.reshape(2, result.shape[1], time_len * CHANNELS).astype(jnp.bfloat16)
    return (dedispersed, bandpass)


def solution(mesh):
    return jax.shard_map(
        on_device,
        mesh=mesh,
        in_specs=(
            P(None, ("stn", "chan"), None, None),
            P(None, ("stn", "chan"), None, None),
            P(("stn", "chan"), None),
            P(("stn", "chan")),
        ),
        out_specs=(P(None, ("stn", "chan"), None), P(("stn", "chan"), None)),
        check_vma=False,
    )
```

profile of v0, /device:TPU:1, one launch (start us, length us, event | category | flops | bytes accessed | tf_op | source)
XLA Modules:
  0.0 83.8 jit_solution(8090392784728288290)
XLA Ops:
  0.6 0.7 fusion.58
  1.4 4.1 %copy_multiply_fusion = bf16[2,8,256,256]{3,1,0,2:T(8,128)(2,1)} fusion(bf16[2,8,256,256]{3,2,1,0:T(8,128)(2,1)} %param.4, bf16[256]{0:T(256)(128)(2,1)S(1)} %select_convert_fusion), kind=kLoop, calls=%fused_computation.26 | loop fusion | flops 1048576 | bytes 4194816 | tf_op jit(solution)/shard_map/mul | solution.py:72
  5.5 11.5 %all-to-all-start = ((bf16[2,8,256,256]{3,1,0,2:T(8,128)(2,1)}), bf16[2,8,256,256]{3,1,0,2:T(8,128)(2,1)S(1)}, u32[]{:S(2)}, u32[]{:S(2)}) async-start(bf16[2,8,256,256]{3,1,0,2:T(8,128)(2,1)} %copy_multiply_fusion), calls=%async_computation | async-start | bytes 4194304 | tf_op jit(solution)/shard_map/all_to_all | solution.py:75
  17.0 1.0 %fusion.57 = bf16[256,1,256]{2,0,1:T(8,128)(2,1)S(1)} fusion(), kind=kLoop, calls=%fused_computation.94 | loop fusion | flops 1048576 | bytes 131072 | tf_op jit(solution)/shard_map/convert.8
  18.0 1.1 %negate_convert_fusion.1 = (bf16[256,1,256]{2,0,1:T(8,128)(2,1)S(1)}, bf16[256,1,256]{2,0,1:T(8,128)(2,1)S(1)}) fusion(), kind=kLoop, calls=%fused_computation.88 | loop fusion | flops 1245184 | bytes 262144 | tf_op jit(solution)/shard_map/convert.4
  19.2 0.8 maximum_bitcast_fusion.6
  20.8 2.3 %maximum_bitcast_fusion.2 = (bf16[2,1,256,2048]{3,2,1,0:T(8,128)(2,1)}, bf16[2,1,256,2048]{3,2,1,0:T(8,128)(2,1)}) fusion(bf16[2,256,1024]{2,1,0:T(8,128)(2,1)S(1)} %fusion.79, bf16[2,256,1024]{2,1,0:T(8,128)(2,1)S(1)} %get-tuple-element.7, bf16[2,256,1024]{2,1,0:T(8,128)(2,1)S(1)} %get-tuple-element.6), kind=kLoop, calls=%fused_computation.24 | loop fusion | flops 8388608 | bytes 7340032 | tf_op jit(solution)/shard_map/stack | solution.py:58
  23.1 12.7 %negate_convert_fusion = (bf16[2,5,256,1,256]{2,4,3,0,1:T(8,128)(2,1)}, bf16[2,5,256,1,256]{2,4,3,0,1:T(8,128)(2,1)}, bf16[2,5,256,1,256]{2,4,3,0,1:T(8,128)(2,1)}) fusion(s32[5,256,256]{1,2,0:T(8,128)S(1)} %fusion.8, s32[2]{0:T(128)S(1)} %broadcast_add_fusion, pred[5,256,256]{1,2,0:T(8,128)(4,1)S(1)} %fusion.11), kind=kLoop, calls=%fused_computation.20 | loop fusion | flops 15073280 | bytes 5570568 | tf_op jit(solution)/shard_map/convert.16
  35.8 10.9 %all-to-all-done = bf16[2,8,256,256]{3,1,0,2:T(8,128)(2,1)S(1)} async-done(((bf16[2,8,256,256]{3,1,0,2:T(8,128)(2,1)}), bf16[2,8,256,256]{3,1,0,2:T(8,128)(2,1)S(1)}, u32[]{:S(2)}, u32[]{:S(2)}) %all-to-all-start) | async-done | bytes 2097184 | tf_op jit(solution)/shard_map/all_to_all | solution.py:75
  46.9 1.4 %copy-done.2 = bf16[2,1,256,2048]{3,2,1,0:T(8,128)(2,1)S(1)} copy-done((bf16[2,1,256,2048]{3,2,1,0:T(8,128)(2,1)S(1)}, bf16[2,1,256,2048]{3,2,1,0:T(8,128)(2,1)}, u32[]{:S(2)}) %copy-start.2) | copy-done | bytes 2097176
  48.3 0.6 copy-done.3
  48.9 1.7 %fusion.21 = bf16[2,256,2,256]{1,3,0,2:T(8,128)(2,1)S(1)} fusion(bf16[2048,2,256,1]{2,0,3,1:T(8,128)(2,1)S(1)} %bitcast.114, bf16[2,1,256,2048]{3,2,1,0:T(8,128)(2,1)S(1)} %copy-done.3, bf16[2,1,256,2048]{3,2,1,0:T(8,128)(2,1)S(1)} %copy-done.2), kind=kOutput, calls=%fused_computation.45 | convolution fusion | flops 1082392576 | bytes 6815744 | tf_op jit(solution)/shard_map/cpbk,kct->pbct/dot_general | solution.py:65
  50.6 1.2 %copy.69 = bf16[2,256,2,256]{3,0,2,1:T(2,128)(2,1)} copy(bf16[2,256,2,256]{1,3,0,2:T(8,128)(2,1)S(1)} %fusion.21) | data formatting | bytes 1048576 | tf_op jit(solution)/shard_map/convert_element_type | solution.py:66
  51.8 4.8 %all-to-all-start.1 = ((bf16[2,256,2,256]{3,0,2,1:T(2,128)(2,1)}), bf16[2,256,2,256]{3,0,2,1:T(2,128)(2,1)S(1)}, u32[]{:S(2)}, u32[]{:S(2)}) async-start(bf16[2,256,2,256]{3,0,2,1:T(2,128)(2,1)} %copy.69), calls=%async_computation.1 | async-start | bytes 1048576 | tf_op jit(solution)/shard_map/all_to_all | solution.py:77
  56.7 3.8 %maximum_bitcast_fusion = (bf16[2,5,1,256,2,256]{3,5,2,4,0,1:T(8,128)(2,1)S(1)}, bf16[2,5,1,256,2,256]{3,5,2,4,0,1:T(8,128)(2,1)}) fusion(bf16[2,5,256,1,256]{2,4,3,0,1:T(8,128)(2,1)} %get-tuple-element.8, bf16[2,5,256,1,256]{2,4,3,0,1:T(8,128)(2,1)} %get-tuple-element.10, bf16[2,5,256,1,256]{2,4,3,0,1:T(8,128)(2,1)} %get-tuple-element.9), kind=kLoop, calls=%fused_computation.18 | loop fusion | flops 2621440 | bytes 9175040 | tf_op jit(solution)/shard_map/vmap()/stack | solution.py:52
  60.5 10.0 %all-to-all-done.1 = bf16[2,256,2,256]{3,0,2,1:T(2,128)(2,1)S(1)} async-done(((bf16[2,256,2,256]{3,0,2,1:T(2,128)(2,1)}), bf16[2,256,2,256]{3,0,2,1:T(2,128)(2,1)S(1)}, u32[]{:S(2)}, u32[]{:S(2)}) %all-to-all-start.1) | async-done | bytes 524320 | tf_op jit(solution)/shard_map/all_to_all | solution.py:77
  70.5 0.8 copy-done.4
  71.3 1.4 %copy.71 = bf16[2,2,128,2,256]{4,1,3,2,0:T(2,128)(2,1)S(1)} copy(bf16[2,2,128,2,256]{4,0,3,1,2:T(2,128)(2,1)} %bitcast.115) | data formatting | bytes 1048576 | tf_op jit(solution)/shard_map/all_to_all | solution.py:77
  72.7 1.1 %copy.72 = bf16[2,2,256,256]{2,3,0,1:T(8,128)(2,1)} copy(bf16[2,2,256,256]{3,1,2,0:T(2,128)(2,1)S(1)} %bitcast.112) | data formatting | bytes 1048576 | tf_op jit(solution)/shard_map/all_to_all | solution.py:77
  74.6 0.7 copy.79
  75.3 1.6 %convolution_bitcast_fusion = f32[2,2,256,256]{3,2,1,0:T(8,128)S(1)} fusion(bf16[1,256,2,256]{3,1,0,2:T(8,128)(2,1)} %get-tuple-element.20, bf16[1,256,2,256]{3,1,0,2:T(8,128)(2,1)S(1)} %get-tuple-element.19, bf16[2,2,256,256]{2,3,0,1:T(8,128)(2,1)} %copy.72), kind=kOutput, calls=%fused_computation.27 | convolution fusion | flops 269484032 | bytes 2097152 | tf_op jit(solution)/shard_map/pbct,pcqk->qbtk/dot_general | solution.py:81
  76.9 1.4 %add_convert_fusion = bf16[2,2,256,256]{3,2,1,0:T(8,128)(2,1)S(1)} fusion(f32[2,2,256,256]{3,2,1,0:T(8,128)S(1)} %convolution_bitcast_fusion, f32[256]{0:T(256)S(1)} %get-tuple-element.22, f32[256]{0:T(256)S(1)} %get-tuple-element.23, f32[256]{0:T(256)S(1)} %get-tuple-element.24, f32[256]{0:T(256)S(1)} %get-tuple-element.25, f32[256]{0:T(256)S(1)} %get-tuple-element.26, ...), kind=kLoop, calls=%fused_computation.57 | loop fusion | flops 6291456 | bytes 1585152 | tf_op jit(solution)/shard_map/convert_element_type | solution.py:93
  80.6 2.1 %fusion.20 = bf16[2,2,256,256]{2,3,0,1:T(8,128)(2,1)S(1)} fusion(f32[2,2,256,256]{3,2,1,0:T(8,128)S(1)} %convolution_bitcast_fusion.1, f32[2,2,256,256]{3,2,1,0:T(8,128)S(1)} %convolution_bitcast_fusion.2, f32[2,2,256,256]{3,2,1,0:T(8,128)S(1)} %convolution_bitcast_fusion.3, f32[2,2,256,256]{3,2,1,0:T(8,128)S(1)} %convolution_bitcast_fusion.4, ...), kind=kOutput, calls=%fused_computation.44 | convolution fusion | flops 276561920 | bytes 11022336 | tf_op jit(solution)/shard_map/pbtu,bpuqa->qbta/dot_general | solution.py:99
  82.9 0.9 %convert_element_type.81 = bf16[2,2,65536]{2,1,0:T(2,128)(2,1)} reshape(bf16[2,2,256,256]{3,2,1,0:T(8,128)(2,1)S(1)} %copy.78) | data formatting | bytes 1048576 | tf_op jit(solution)/shard_map/convert_element_type | solution.py:105
  (29 shorter events, 4.4 us)
Async XLA Ops:
  5.5 13.6 %copy-start.5 = (s32[2]{0:T(128)S(1)}, s32[2]{0:T(128)}, u32[]{:S(2)}) copy-start(s32[2]{0:T(128)} %param.7) | copy-start | bytes 28
  5.5 41.2 %all-to-all-start = ((bf16[2,8,256,256]{3,1,0,2:T(8,128)(2,1)}), bf16[2,8,256,256]{3,1,0,2:T(8,128)(2,1)S(1)}, u32[]{:S(2)}, u32[]{:S(2)}) async-start(bf16[2,8,256,256]{3,1,0,2:T(8,128)(2,1)} %copy_multiply_fusion), calls=%async_computation | async-start | bytes 4194304 | tf_op jit(solution)/shard_map/all_to_all | solution.py:75
  17.0 3.5 %copy-start.1 = (bf16[2,2,256,1024]{3,2,1,0:T(8,128)(2,1)S(1)}, bf16[2,2,256,1024]{3,2,1,0:T(8,128)(2,1)}, u32[]{:S(2)}) copy-start(bf16[2,2,256,1024]{3,2,1,0:T(8,128)(2,1)} %param.5) | copy-start | bytes 6291460
  46.7 1.6 %copy-start.2 = (bf16[2,1,256,2048]{3,2,1,0:T(8,128)(2,1)S(1)}, bf16[2,1,256,2048]{3,2,1,0:T(8,128)(2,1)}, u32[]{:S(2)}) copy-start(bf16[2,1,256,2048]{3,2,1,0:T(8,128)(2,1)} %get-tuple-element.13) | copy-start | bytes 6291460
  46.7 2.2 %copy-start.3 = (bf16[2,1,256,2048]{3,2,1,0:T(8,128)(2,1)S(1)}, bf16[2,1,256,2048]{3,2,1,0:T(8,128)(2,1)}, u32[]{:S(2)}) copy-start(bf16[2,1,256,2048]{3,2,1,0:T(8,128)(2,1)} %get-tuple-element.14) | copy-start | bytes 6291460
  51.8 18.7 %all-to-all-start.1 = ((bf16[2,256,2,256]{3,0,2,1:T(2,128)(2,1)}), bf16[2,256,2,256]{3,0,2,1:T(2,128)(2,1)S(1)}, u32[]{:S(2)}, u32[]{:S(2)}) async-start(bf16[2,256,2,256]{3,0,2,1:T(2,128)(2,1)} %copy.69), calls=%async_computation.1 | async-start | bytes 1048576 | tf_op jit(solution)/shard_map/all_to_all | solution.py:77
  70.5 0.8 copy-start.4
  76.8 1.8 %copy-start = (bf16[2,5,1,256,2,256]{3,5,2,4,0,1:T(8,128)(2,1)S(1)}, bf16[2,5,1,256,2,256]{3,5,2,4,0,1:T(8,128)(2,1)}, u32[]{:S(2)}) copy-start(bf16[2,5,1,256,2,256]{3,5,2,4,0,1:T(8,128)(2,1)} %get-tuple-element.12) | copy-start | bytes 7864324
where the time goes:
time: 84.1 us; the launch traced here: 83.8 us
  other arithmetic  29.5 us (35%)
  waiting for transfers between devices  20.9 us (25%)
  starting transfers between devices  16.3 us (19%)
  local copies, waits for them, and re-layouts  9.12 us (11%)
  matrix products  7.21 us (9%)
    another operation x3, other arithmetic  14.8 us
    all_to_all x1, starting transfers between devices, on_device(): lax.all_to_all(outgoing, ('stn', 'chan'), split_axis=2, concat_axis=1, ti...  11.5 us
    all_to_all x1, waiting for transfers between devices, on_device(): lax.all_to_all(outgoing, ('stn', 'chan'), split_axis=2, concat_axis=1, ti...  10.9 us
    all_to_all x1, waiting for transfers between devices, on_device(): lax.all_to_all(beams, ('stn', 'chan'), split_axis=1, concat_axis=2, tiled...  10 us
    all_to_all x1, starting transfers between devices, on_device(): lax.all_to_all(beams, ('stn', 'chan'), split_axis=1, concat_axis=2, tiled...  4.76 us
    mul x1, other arithmetic, on_device(): outgoing = voltages * keep[None, :, :, None].astype(jnp.bfloat16)  4.11 us
    dot_general x5, matrix products, on_device(): jnp.einsum('pbtu,bpuqa->qbta', longer[:, :, blk:blk + time_len, :], table...  3.97 us
    another operation x1, other arithmetic, chirp_table(): return jnp.stack([from_real, from_imag], axis=1).astype(jnp.bfloat16)  3.81 us
  transfers between devices with their start and end apart: 2, of which 2 were waited for; matrix products, arithmetic and copies ran while one was open for 27% of the time, Pallas kernels for 0%

commit v1 on v0

v1 whole, which is shorter than its diff:
```python
import math
import random

import jax
import jax.numpy as jnp
import numpy as np
from jax import lax
from jax.experimental import pallas as pl
from jax.experimental.pallas import tpu as pltpu
from jax.sharding import PartitionSpec as P

CHANNELS = 256
BEAMS = 256
INPUTS = 1024
TIME = 256
TAPS = 12
CHIRP = 1024
DMS = 16
NBLOCK = CHIRP // CHANNELS + 1
DEVICES = 128
CHAN_AXIS = 16
MESH = pl.DeviceIdType.MESH
BF16 = jnp.bfloat16
F32 = jnp.float32


def dft_rows():
    order = np.arange(CHANNELS)
    angle = 2.0 * math.pi / CHANNELS * (order[:, None] * order[None, :] % CHANNELS)
    cosine = np.cos(angle) / math.sqrt(CHANNELS)
    sine = np.sin(angle) / math.sqrt(CHANNELS)
    return np.block([[cosine, sine], [-sine, cosine]]).astype(np.float32)


def prototype():
    counter = np.arange(TAPS * CHANNELS, dtype=np.float64)
    offset = (counter + 0.5) / CHANNELS - TAPS / 2.0
    window = 0.54 + 0.46 * np.cos(math.pi * offset / (TAPS / 2.0))
    taps = (np.sinc(offset) * window).reshape(TAPS, CHANNELS)
    return np.concatenate([taps, taps], axis=1).astype(np.float32)


def chirp_rows():
    dms = np.arange(DMS, dtype=np.int64)[:, None, None]
    lag = np.arange(NBLOCK)[None, :, None] * CHANNELS + CHANNELS - 1 - np.arange(2 * CHANNELS)[None, None, :]
    valid = (lag >= 0) & (lag < CHIRP)
    lag = np.clip(lag, 0, CHIRP - 1)
    angle = math.pi * ((dms + 1) * lag * lag % (2 * DMS * CHIRP)) / (DMS * CHIRP)
    real = np.where(valid, np.cos(angle), 0.0) / math.sqrt(CHIRP)
    imag = np.where(valid, np.sin(angle), 0.0) / math.sqrt(CHIRP)
    rows = np.concatenate([real, imag, np.zeros((DMS, 6, 2 * CHANNELS))], axis=1)
    return rows.astype(np.float32)


def iota(axis, shape=(256, 256)):
    return lax.broadcasted_iota(jnp.int32, shape, axis)


def ones_where(condition):
    return jnp.where(condition, 1.0, 0.0).astype(BF16)


def dot(a, b):
    return jnp.dot(a, b, preferred_element_type=F32)


def exchange_order():
    steps = [(dz, one, dx) for dz in range(4) for one in range(2) for dx in range(4)]
    random.Random(7).shuffle(steps)
    mixed = []
    for dz, one, dx in steps:
        for step in ((dz, one, dx), (-dz % 4, 1 - one, -dx % 4)):
            if step not in mixed:
                mixed.append(step)
    return mixed


def body(
    volt, wgt, flags, dm, chirps, recv2, tables,
    vin, send, recv, win, toep, chv, flagv, dmv, acc, send2, keep,
    load_sem, table_sem, sent, sent2, recv_sem, recv_sem2, plane_sem,
):
    x = lax.rem(lax.axis_index("chan"), 4)
    y = lax.axis_index("chan") // 4
    z = lax.axis_index("stn") // 2
    core = lax.rem(lax.axis_index("stn"), 2)
    me = lax.axis_index("stn") * CHAN_AXIS + lax.axis_index("chan")

    turn = 1 + 2 * core
    zs = [lax.rem(z + dz * turn, 4) * 2 for dz in range(4)]
    xs = [lax.rem(x + dx * turn, 4) for dx in range(4)]
    ys = [lax.rem(y + dy, 4) * 4 for dy in range(4)]
    cores = (core, 1 - core)
    batches = [(other, lax.rem(y // 2 + k + core, 2)) for other in range(2) for k in range(2)]

    flag_load = pltpu.make_async_copy(flags, flagv, load_sem.at[4])
    flag_load.start()
    volt_loads = [
        pltpu.make_async_copy(volt.at[:, :, cores[other], half], vin.at[:, :, cores[other], half], load_sem.at[n])
        for n, (other, half) in enumerate(batches)
    ]
    for load in volt_loads:
        load.start()

    barrier = pltpu.get_barrier_semaphore()
    greeted = [(zs[dz] + core, ys[0] + x) for dz in range(1, 4)]
    line = list(greeted)
    for other in range(2):
        for dy in range(4):
            for dx in range(4):
                if (other, dy, dx) != (0, 0, 0):
                    greeted.append((zs[0] + cores[other], ys[dy] + xs[dx]))
    for place in greeted:
        pl.semaphore_signal(barrier, inc=1, device_id=place, device_id_type=MESH)

    def send_batch(n, send, landing, sent, recv_sem):
        other, half = batches[n]
        for dz, one, dx in exchange_order():
            stn, yy = zs[dz] + cores[other], half * 2 + one
            chan = yy * 4 + xs[dx]

            def away():
                pltpu.make_async_remote_copy(
                    src_ref=send.at[stn * CHAN_AXIS + chan],
                    dst_ref=landing(me),
                    send_sem=sent,
                    recv_sem=recv_sem.at[other],
                    device_id=(stn, chan),
                    device_id_type=MESH,
                ).start()

            if (other, dz, dx) == (0, 0, 0):
                pl.when(yy != y)(away)

                @pl.when(yy == y)
                def _():
                    pltpu.make_async_copy(send.at[me], landing(me), recv_sem.at[0]).start()
            else:
                away()

    flag_load.wait()
    row, col = iota(0), iota(1)
    hits = ones_where(iota(0, (256, 64)) == flagv[...])
    count = dot(hits, jnp.ones((64, 256), BF16))
    keep_rows = ones_where((count < 0.5) & (row % 16 == col % 16))
    keep[...] = dot(ones_where(iota(1, (16, 256)) // 16 == iota(0, (16, 256))), keep_rows)

    there = (row // 32) * 2 + (row // 8) % 2
    swap = jnp.where((col // 16 == ((row // 16) % 2) * 8 + row % 8) & (col % 16 == there), 1.0, 0.0)

    pl.semaphore_wait(barrier, len(greeted))
    for place in line:
        pl.semaphore_signal(plane_sem, inc=1, device_id=place, device_id_type=MESH)
    loads = [
        pltpu.make_async_copy(source, target, load_sem.at[n])
        for n, (source, target) in enumerate(((wgt, win), (dm, dmv), (chirps, chv)), 5)
    ]
    for n, (other, half) in enumerate(batches):
        volt_loads[n].wait()
        for plane in range(4):
            g = (plane * 2 + cores[other]) * 2 + half
            block = vin[:, plane, cores[other], half].reshape(256, 256)
            mine = (swap * keep[pl.ds(g, 1), :]).astype(BF16)
            send[pl.ds(pl.multiple_of(g * 8, 8), 8)] = dot(mine, block).astype(BF16).reshape(8, 4, 8, 256)
        if n == 0:
            for load in loads:
                load.start()
            pl.semaphore_wait(plane_sem, len(line))
        send_batch(n, send, lambda source: recv.at[:, source], sent, recv_sem)

    for load in loads:
        load.wait()

    def toeplitz(row_of):
        wide = jnp.broadcast_to(row_of, (CHANNELS, 2 * CHANNELS))
        rolled = pltpu.roll(wide, CHANNELS + 1, 1, stride=1, stride_axis=0)
        return rolled[:, :CHANNELS]

    for b in range(2):
        chosen = chv[dmv[b]]
        for blk in range(NBLOCK):
            real = toeplitz(chosen[blk : blk + 1])
            imag = toeplitz(chosen[NBLOCK + blk : NBLOCK + blk + 1])
            upper = jnp.concatenate([real, -imag], axis=1).astype(BF16)
            lower = jnp.concatenate([imag, real], axis=1).astype(BF16)
            toep[b, blk * 512 : blk * 512 + 256, :] = upper
            toep[b, blk * 512 + 256 : blk * 512 + 512, :] = lower
    table_store = pltpu.make_async_copy(toep, tables, table_sem)
    table_store.start()

    for other in range(2):
        half = recv.at[:, pl.ds(0, 64)]
        pltpu.make_async_copy(half, half, recv_sem.at[other]).wait()
        stn_core = lax.rem(core + other, 2)
        for c in range(2):
            real, imag, weight_real, weight_imag = [], [], [], []
            for plane in range(4):
                stn = 2 * plane + stn_core
                sources = pl.ds(pl.multiple_of(stn * 16, 16), 16)
                inputs = pl.ds(pl.multiple_of(stn * 128, 128), 128)
                real.append(recv[c, sources].reshape(128, 256))
                imag.append(recv[2 + c, sources].reshape(128, 256))
                weight_real.append(win[0, c, :, inputs])
                weight_imag.append(win[1, c, :, inputs])
            real, imag = jnp.concatenate(real, axis=0), jnp.concatenate(imag, axis=0)
            both = jnp.concatenate(weight_real + weight_imag, axis=1)
            parts = jnp.concatenate(
                [jnp.concatenate([real, imag], axis=1), jnp.concatenate([-imag, real], axis=1)], axis=0
            )
            if other == 0:
                acc[c] = dot(both, parts)
            else:
                acc[c] += dot(both, parts)

    order = ones_where(
        (col // 128 == row % 2) & ((col // 64) % 2 == (row // 2) % 2) & (col % 64 == (row // 8) * 2 + (row // 4) % 2)
    )
    for m in range(4):
        rows = slice(m * 64, m * 64 + 64)
        block = jnp.concatenate([acc[c, rows, q * 256 : q * 256 + 256] for c in range(2) for q in range(2)], axis=0)
        block = dot(order, block.astype(BF16)).astype(BF16)
        send2[m * 32 : m * 32 + 32] = block.reshape(32, 8, 256)
    for n in range(4):
        send_batch(n, send2, lambda source: recv2.at[source], sent2, recv_sem2)
    table_store.wait()
    blocks = send.at[pl.ds(0, DEVICES - 1)]
    pltpu.make_async_copy(blocks, blocks, sent).wait()
    blocks = send2.at[pl.ds(0, DEVICES - 1)]
    pltpu.make_async_copy(blocks, blocks, sent2).wait()
    for other in range(2):
        half = recv2.at[pl.ds(0, 64)]
        pltpu.make_async_copy(half, half, recv_sem2.at[other]).wait()


def tail(beams, tables, dft, proto, out, band, xv, xs, tv, dftv, protov, padded, even, odd, load_sem):
    loads = [
        pltpu.make_async_copy(source, target, load_sem.at[n])
        for n, (source, target) in enumerate(((beams, xv), (dft, dftv), (proto, protov), (tables, tv)))
    ]
    for load in loads:
        load.start()
    row, col = iota(0), iota(1)
    sort = ones_where(col == ((row % 64) // 2) * 8 + (row // 64) * 2 + row % 2)
    spread = ones_where(col == (row % 8) * 32 + row // 8)
    loads[0].wait()
    for n in range(4):
        block = dot(sort, xv[n * 256 : n * 256 + 256, :]).astype(BF16)
        for k in range(4):
            xs[k // 2, (k % 2) * 256 + n * 64 : (k % 2) * 256 + n * 64 + 64, :] = block[k * 64 : k * 64 + 64]
    loads[1].wait()
    loads[2].wait()
    for b in range(2):
        turned = lax.dot_general(spread, xs[b], (((1,), (1,)), ((), ())), preferred_element_type=F32)
        power = jnp.sum(turned * turned, axis=0, keepdims=True) * (1.0 / TIME)
        band[b : b + 1, :] = power[:, :256] + power[:, 256:]
        spectra = dot(turned.astype(BF16), dftv[...])
        before = pltpu.roll(spectra[168:], 1, 0)
        padded[b, 0:88, :] = jnp.where(iota(0, (88, 512)) % 8 == 0, 0.0, before)
        padded[b, 88:344, :] = spectra
    for b in range(2):
        for n in range(4):
            lanes = slice(n * 128, n * 128 + 128)
            series = protov[0:1, lanes] * padded[b, 88:344, lanes]
            for tap in range(1, TAPS):
                series = series + protov[tap : tap + 1, lanes] * padded[b, 88 - 8 * tap : 344 - 8 * tap, lanes]
            after = pltpu.roll(series[:32], 31, 0)
            after = jnp.where(iota(0, (32, 128)) % 8 == 7, 0.0, after)
            even[b, 0:256, lanes] = series.astype(BF16)
            even[b, 256:288, lanes] = after.astype(BF16)
            odd[b, 0:272, lanes] = jnp.concatenate([series[8:], after[:24]], axis=0).astype(BF16)
    loads[3].wait()
    results = []
    for b in range(2):
        lhs = jnp.concatenate(
            [even[b, 0:256], odd[b, 0:256], even[b, 16:272], odd[b, 16:272], even[b, 32:288]], axis=1
        )
        results.append(dot(lhs, tv[b]).astype(BF16))
    final = ones_where(col == (row % 4) * 64 + ((row // 4) % 8) * 8 + row // 32)
    for j in range(4):
        rows = slice(64 * j, 64 * j + 64)
        block = jnp.concatenate(
            [
                jnp.concatenate([results[b][rows, half * 128 + q * 256 : half * 128 + q * 256 + 128] for q in range(2)], axis=1)
                for half in range(2) for b in range(2)
            ],
            axis=0,
        )
        block = dot(final, block).astype(BF16)
        for q in range(2):
            for k in range(8):
                out[q, 128 * k + 32 * j : 128 * k + 32 * j + 32, :] = block[32 * k : 32 * k + 32, q * 128 : q * 128 + 128]


def on_device(voltages, weights, flags, dm_index):
    hbm = pl.BlockSpec(memory_space=pl.ANY)
    vmem = pl.BlockSpec(memory_space=pltpu.VMEM)
    dma = pltpu.SemaphoreType.DMA
    params = dict(vmem_limit_bytes=62 * 1024 * 1024)
    beams, tables = pl.pallas_call(
        body,
        out_shape=(
            jax.ShapeDtypeStruct((DEVICES, 8, 256), BF16),
            jax.ShapeDtypeStruct((2, NBLOCK * 512, 512), BF16),
        ),
        in_specs=[hbm] * 5,
        out_specs=(hbm, hbm),
        scratch_shapes=[
            pltpu.VMEM((16, 4, 2, 2, 16, 256), BF16),
            pltpu.VMEM((DEVICES, 4, 8, 256), BF16),
            pltpu.VMEM((4, DEVICES, 8, 256), BF16),
            pltpu.VMEM((2, 2, 256, 1024), BF16),
            pltpu.VMEM((2, NBLOCK * 512, 512), BF16),
            pltpu.VMEM((DMS, 16, 512), F32),
            pltpu.VMEM((1, 64), jnp.int32),
            pltpu.SMEM((2,), jnp.int32),
            pltpu.VMEM((2, 256, 512), F32),
            pltpu.VMEM((DEVICES, 8, 256), BF16),
            pltpu.VMEM((16, 256), F32),
            dma((8,)),
            dma,
            dma,
            dma,
            dma((2,)),
            dma((2,)),
            pltpu.SemaphoreType.REGULAR,
        ],
        compiler_params=pltpu.CompilerParams(collective_id=0, has_side_effects=True, **params),
        name="beamform",
    )(
        voltages.reshape(16, 4, 2, 2, 16, TIME),
        weights,
        flags,
        dm_index,
        jnp.asarray(chirp_rows()).astype(BF16).astype(F32),
    )
    dedispersed, bandpass = pl.pallas_call(
        tail,
        out_shape=(
            jax.ShapeDtypeStruct((2, 2 * TIME * 2, 128), BF16),
            jax.ShapeDtypeStruct((2, CHANNELS), F32),
        ),
        in_specs=[hbm] * 4,
        out_specs=(vmem, vmem),
        scratch_shapes=[
            pltpu.VMEM((1024, 256), BF16),
            pltpu.VMEM((2, 512, 256), BF16),
            pltpu.VMEM((2, NBLOCK * 512, 512), BF16),
            pltpu.VMEM((512, 512), BF16),
            pltpu.VMEM((TAPS, 512), F32),
            pltpu.VMEM((2, 344, 512), F32),
            pltpu.VMEM((2, 288, 512), BF16),
            pltpu.VMEM((2, 272, 512), BF16),
            dma((4,)),
        ],
        compiler_params=pltpu.CompilerParams(**params),
        name="synthesis",
    )(
        beams.reshape(1024, 256),
        tables,
        jnp.asarray(dft_rows()).astype(BF16),
        jnp.asarray(prototype()),
    )
    dedispersed = dedispersed.reshape(2, 512, 2, 128).transpose(0, 2, 1, 3).reshape(2, 2, TIME * CHANNELS)
    return dedispersed, bandpass


def solution(mesh):
    return jax.shard_map(
        on_device,
        mesh=mesh,
        in_specs=(
            P(None, ("stn", "chan"), None, None),
            P(None, ("stn", "chan"), None, None),
            P(("stn", "chan"), None),
            P(("stn", "chan")),
        ),
        out_specs=(P(None, ("stn", "chan"), None), P(("stn", "chan"), None)),
        check_vma=False,
    )
```

time: 84.1 us -> 54.6 us (0.65)
  Pallas kernels: 0 us -> 53.9 us
  other arithmetic: 29.5 us -> 0 us
  waiting for transfers between devices: 20.9 us -> 0 us
  starting transfers between devices: 16.3 us -> 0 us
  local copies, waits for them, and re-layouts: 9.12 us -> 0 us
  matrix products: 7.21 us -> 0 us
    pallas_call x0 -> x2, Pallas kernels: none -> 53.9 us  [the longest x1 48.1 us: on_device(): pl.pallas_call(body, out_shape=(jax.ShapeDtypeStruct((DEVICES, 8, 256), B...]
    another operation x6 -> x0, other arithmetic: 21.7 us -> none
    all_to_all x2 -> x0, waiting for transfers between devices: 20.9 us -> none  [the longest x1 10.9 us: on_device(): lax.all_to_all(outgoing, ('stn', 'chan'), split_axis=2, concat_axis=1, ti...]
    all_to_all x2 -> x0, starting transfers between devices: 16.3 us -> none  [the longest x1 11.5 us: on_device(): lax.all_to_all(outgoing, ('stn', 'chan'), split_axis=2, concat_axis=1, ti...]
    dot_general x7 -> x0, matrix products: 7.21 us -> none  [the longest x5 3.97 us: on_device(): jnp.einsum('pbtu,bpuqa->qbta', longer[:, :, blk:blk + time_len, :], table...]
    mul x3 -> x0, other arithmetic: 4.19 us -> none  [the longest x1 4.11 us: on_device(): outgoing = voltages * keep[None, :, :, None].astype(jnp.bfloat16)]
    unnamed x13 -> x0, local copies, waits for them, and re-layouts: 3.55 us -> none
    all_to_all x3 -> x0, local copies, waits for them, and re-layouts: 2.67 us -> none  [the longest x2 2.54 us: on_device(): lax.all_to_all(beams, ('stn', 'chan'), split_axis=1, concat_axis=2, tiled...]
  transfers between devices with their start and end apart: 2 -> 0, of which waited for: 2 -> 0; matrix products, arithmetic and copies ran while one was open for 27% -> 0% of each run, Pallas kernels for 0% -> 0%
where the time goes in v1:
time: 54.6 us; the launch traced here: 54.5 us
  Pallas kernels  53.9 us (99%)
  between operations  0.64 us (1%)
    pallas_call x1, Pallas kernels, on_device(): pl.pallas_call(body, out_shape=(jax.ShapeDtypeStruct((DEVICES, 8, 256), B...  48.1 us
    pallas_call x1, Pallas kernels, on_device(): pl.pallas_call(tail, out_shape=(jax.ShapeDtypeStruct((2, 2 * TIME * 2, 12...  5.72 us

profile of v1, /device:TPU:1, one launch (start us, length us, event | category | flops | bytes accessed | tf_op | source)
XLA Modules:
  0.0 54.5 jit_solution(15683943127155243373)
XLA Ops:
  0.6 48.1 %beamform.1 = (bf16[128,8,256]{2,1,0:T(8,128)(2,1)}, bf16[2,2560,512]{2,1,0:T(8,128)(2,1)}) custom-call(bf16[16,4,2,2,16,256]{5,4,3,2,1,0:T(8,128)(2,1)} %bitcast.7, bf16[2,2,256,1024]{3,2,1,0:T(8,128)(2,1)} %wgt.1, s32[1,64]{1,0:T(1,128)} %flags.1, s32[2]{0:T(128)} %dm.1, f32[16,16,512]{2,1,0:T(8,128)} %constant.14.chirps), custom_call_target="tpu_custom_call" | custom-call | tf_op jit(solution)/shard_map/beamform/pallas_call | solution.py:299
  48.8 5.7 %synthesis.1 = (bf16[2,1024,128]{2,1,0:T(8,128)(2,1)}, f32[2,256]{1,0:T(2,128)}) custom-call(bf16[1024,256]{1,0:T(8,128)(2,1)} %bitcast.8, bf16[2,2560,512]{2,1,0:T(8,128)(2,1)} %get-tuple-element.7.tables, bf16[512,512]{1,0:T(8,128)(2,1)} %constant.15.dft, f32[12,512]{1,0:T(8,128)} %constant.8.clone.proto), custom_call_target="tpu_custom_call" | custom-call | tf_op jit(solution)/shard_map/synthesis/pallas_call | solution.py:336

commit v2 on v1

v2 whole, which is shorter than its diff:
```python
import math
import random

import jax
import jax.numpy as jnp
import numpy as np
from jax import lax
from jax.experimental import pallas as pl
from jax.experimental.pallas import tpu as pltpu
from jax.sharding import PartitionSpec as P

CHANNELS = 256
BEAMS = 256
INPUTS = 1024
TIME = 256
TAPS = 12
CHIRP = 1024
DMS = 16
NBLOCK = CHIRP // CHANNELS + 1
DEVICES = 128
CHAN_AXIS = 16
PARTS = 2
SPAN = TIME // PARTS
MESH = pl.DeviceIdType.MESH
BF16 = jnp.bfloat16
F32 = jnp.float32


def dft_rows():
    order = np.arange(CHANNELS)
    angle = 2.0 * math.pi / CHANNELS * (order[:, None] * order[None, :] % CHANNELS)
    cosine = np.cos(angle) / math.sqrt(CHANNELS)
    sine = np.sin(angle) / math.sqrt(CHANNELS)
    return np.block([[cosine, sine], [-sine, cosine]]).astype(np.float32)


def prototype():
    counter = np.arange(TAPS * CHANNELS, dtype=np.float64)
    offset = (counter + 0.5) / CHANNELS - TAPS / 2.0
    window = 0.54 + 0.46 * np.cos(math.pi * offset / (TAPS / 2.0))
    taps = (np.sinc(offset) * window).reshape(TAPS, CHANNELS)
    return np.concatenate([taps, taps], axis=1).astype(np.float32)


def chirp_rows():
    dms = np.arange(DMS, dtype=np.int64)[:, None, None]
    lag = np.arange(NBLOCK)[None, :, None] * CHANNELS + CHANNELS - 1 - np.arange(2 * CHANNELS)[None, None, :]
    valid = (lag >= 0) & (lag < CHIRP)
    lag = np.clip(lag, 0, CHIRP - 1)
    angle = math.pi * ((dms + 1) * lag * lag % (2 * DMS * CHIRP)) / (DMS * CHIRP)
    real = np.where(valid, np.cos(angle), 0.0) / math.sqrt(CHIRP)
    imag = np.where(valid, np.sin(angle), 0.0) / math.sqrt(CHIRP)
    rows = np.concatenate([real, imag, np.zeros((DMS, 6, 2 * CHANNELS))], axis=1)
    return rows.astype(np.float32)


def iota(axis, shape=(256, 256)):
    return lax.broadcasted_iota(jnp.int32, shape, axis)


def ones_where(condition):
    return jnp.where(condition, 1.0, 0.0).astype(BF16)


def dot(a, b):
    return jnp.dot(a, b, preferred_element_type=F32)


def exchange_order():
    left = [(dz, dy, dx) for dz in range(4) for dy in range(4) for dx in range(4)]
    random.Random(7).shuffle(left)
    hops, ordered = [0, 0, 0], []
    while left:
        def uneven(step):
            return sum((done + min(d, 4 - d) - len(ordered) - 1) ** 2 for done, d in zip(hops, step))

        best = min(left, key=uneven)
        left.remove(best)
        ordered.append(best)
        hops = [done + min(d, 4 - d) for done, d in zip(hops, best)]
    return ordered


def body(
    volt, wgt, flags, dm, chirps, dft, proto, recv2, tables, dftv, protov,
    vin, give, send, recv, win, chv, flagv, dmv, beams, give2, send2, keep,
    load_sem, plane_sem, given, given2, sent, sent2, sibling_sem, sibling_sem2, recv_sem, recv_sem2,
):
    x = lax.rem(lax.axis_index("chan"), 4)
    y = lax.axis_index("chan") // 4
    z = lax.axis_index("stn") // 2
    core = lax.rem(lax.axis_index("stn"), 2)
    chip = z * CHAN_AXIS + lax.axis_index("chan")
    sibling = (z * 2 + 1 - core, lax.axis_index("chan"))

    turn = 1 + 2 * core
    zs = [lax.rem(z + dz * turn, 4) for dz in range(4)]
    xs = [lax.rem(x + dx * turn, 4) for dx in range(4)]
    ys = [lax.rem(y + dy * turn, 4) * 4 for dy in range(4)]

    flag_load = pltpu.make_async_copy(flags, flagv, load_sem.at[0])
    flag_load.start()
    volt_loads = [
        pltpu.make_async_copy(volt.at[:, :, number], vin.at[:, :, number], load_sem.at[n])
        for n, number in ((1, 1 - core), (2, core))
    ]
    for load in volt_loads:
        load.start()

    barrier = pltpu.get_barrier_semaphore()
    line = [(zs[dz] * 2 + core, ys[0] + x) for dz in range(1, 4)]
    plane = [(z * 2 + core, ys[dy] + xs[dx]) for dy in range(4) for dx in range(4) if (dy, dx) != (0, 0)]
    greeted = [sibling] + line + plane
    for place in greeted:
        pl.semaphore_signal(barrier, inc=1, device_id=place, device_id_type=MESH)

    def hand_over(part, give, send, given, sibling_sem):
        pltpu.make_async_remote_copy(
            src_ref=give.at[part],
            dst_ref=send.at[part, :, core],
            send_sem=given,
            recv_sem=sibling_sem.at[part],
            device_id=sibling,
            device_id_type=MESH,
        ).start()

    def exchange(part, send, landing, sibling_sem, sent, recv_sem):
        share = send.at[part, :, 1 - core]
        pltpu.make_async_copy(share, share, sibling_sem.at[part]).wait()
        pltpu.make_async_copy(send.at[part, chip], landing, recv_sem.at[part]).start()
        for dz, dy, dx in exchange_order():
            if (dz, dy, dx) != (0, 0, 0):
                chan = ys[dy] + xs[dx]
                pltpu.make_async_remote_copy(
                    src_ref=send.at[part, zs[dz] * CHAN_AXIS + chan],
                    dst_ref=landing,
                    send_sem=sent.at[part],
                    recv_sem=recv_sem.at[part],
                    device_id=(zs[dz] * 2 + core, chan),
                    device_id_type=MESH,
                ).start()

    flag_load.wait()
    row, col = iota(0), iota(1)
    hits = ones_where(iota(0, (256, 64)) == flagv[...])
    count = dot(hits, jnp.ones((64, 256), BF16))
    keep_rows = ones_where((count < 0.5) & (row % 16 == col % 16))
    keep[...] = dot(ones_where(iota(1, (16, 256)) // 16 == iota(0, (16, 256))), keep_rows)

    there = (row // 32) * 2 + (row // 8) % 2
    swap = jnp.where((col // 16 == ((row // 16) % 2) * 8 + row % 8) & (col % 16 == there), 1.0, 0.0)

    def sort_out(number):
        for zz in range(4):
            for half in range(2):
                block = vin[:, zz, number, half].reshape(256, 256)
                mine = (swap * keep[pl.ds((zz * 2 + number) * 2 + half, 1), :]).astype(BF16)
                yield slice(zz * 16 + half * 8, zz * 16 + half * 8 + 8), dot(mine, block).astype(BF16).reshape(8, 4, 8, 256)

    volt_loads[0].wait()
    for chips, block in sort_out(1 - core):
        for part in range(PARTS):
            give[part, chips] = block[..., part * SPAN : part * SPAN + SPAN]
    pl.semaphore_wait(barrier, len(greeted))
    for place in line:
        pl.semaphore_signal(plane_sem, inc=1, device_id=place, device_id_type=MESH)
    for part in range(PARTS):
        hand_over(part, give, send, given, sibling_sem)
    volt_loads[1].wait()
    for chips, block in sort_out(core):
        for part in range(PARTS):
            send[part, chips, core] = block[..., part * SPAN : part * SPAN + SPAN]
    loads = [
        pltpu.make_async_copy(source, target, load_sem.at[n])
        for n, (source, target) in enumerate(
            ((wgt, win), (dm, dmv), (chirps, chv), (dft, dftv), (proto, protov)), 3
        )
    ]
    for load in loads:
        load.start()
    pl.semaphore_wait(plane_sem, len(line))
    for part in range(PARTS):
        exchange(part, send, recv.at[part, chip], sibling_sem, sent, recv_sem)
    for load in loads:
        load.wait()

    def toeplitz(n, carry):
        b, block = n // NBLOCK, lax.rem(n, NBLOCK)
        for part in range(2):
            wide = jnp.broadcast_to(chv[dmv[b], pl.ds(part * NBLOCK + block, 1), :], (8, 2 * CHANNELS))
            eight = pltpu.roll(wide, CHANNELS + 1, 1, stride=1, stride_axis=0)
            for k in range(0, CHANNELS, 16):
                both = [pltpu.roll(eight, k + i, 1)[:, :CHANNELS] if k + i else eight[:, :CHANNELS] for i in (0, 8)]
                rows = pl.ds(pl.multiple_of(block * CHANNELS + k, 16), 16)
                tables[b, rows, part * CHANNELS : (part + 1) * CHANNELS] = jnp.concatenate(both, axis=0).astype(BF16)
        return carry

    lax.fori_loop(0, 2 * NBLOCK, toeplitz, 0)

    to_device = lax.rem(core + row // 128, 2) * 16 + (row // 8) % 16
    order = ones_where(
        (col // 128 == row % 2) & ((col // 64) % 2 == (row // 2) % 2) & (col % 64 == to_device * 2 + (row // 4) % 2)
    )
    for part in range(PARTS):
        arrived = recv.at[part]
        pltpu.make_async_copy(arrived, arrived, recv_sem.at[part]).wait()
        for c in range(2):
            both, real, imag = [], [], []
            for number in range(2):
                real.append(recv[part, :, number, c].reshape(512, SPAN))
                imag.append(recv[part, :, number, 2 + c].reshape(512, SPAN))
            for p in range(2):
                for number in range(2):
                    for zz in range(4):
                        inputs = (zz * 2 + number) * 128
                        both.append(win[p, c, :, inputs : inputs + 128])
            parts = jnp.concatenate(
                [
                    jnp.concatenate(real + [-half for half in imag], axis=0),
                    jnp.concatenate(imag + real, axis=0),
                ],
                axis=1,
            )
            beams[c] = dot(jnp.concatenate(both, axis=1), parts).astype(BF16)
        for zz in range(4):
            rows = slice(zz * 64, zz * 64 + 64)
            block = jnp.concatenate([beams[c, rows, q * SPAN : q * SPAN + SPAN] for c in range(2) for q in range(2)], axis=0)
            block = dot(order, block).astype(BF16)
            send2[part, zz * 16 : zz * 16 + 16, core] = block[:128].reshape(16, 8, SPAN)
            give2[part, zz * 16 : zz * 16 + 16] = block[128:].reshape(16, 8, SPAN)
        hand_over(part, give2, send2, given2, sibling_sem2)
        exchange(part, send2, recv2.at[part, chip], sibling_sem2, sent2, recv_sem2)

    for blocks, sem in ((give, given), (give2, given2)):
        pltpu.make_async_copy(blocks, blocks, sem).wait()
    for part in range(PARTS):
        for blocks, sem in ((send.at[part, 0:63], sent), (send2.at[part, 0:63], sent2), (recv2.at[part], recv_sem2)):
            pltpu.make_async_copy(blocks, blocks, sem.at[part]).wait()


def tail(xv, tv, dftv, protov, out, band, xs, padded0, padded1, even0, even1, odd0, odd1):
    row, col = iota(0), iota(1)
    sort = ones_where(col == ((row % 32) // 2 * 2 + (row % 64) // 32) * 8 + (row // 64) * 2 + row % 2)
    spread = ones_where(col == (row % 8) * 32 + row // 8)
    for part in range(PARTS):
        for n in range(4):
            block = dot(sort, xv[part, n * 256 : n * 256 + 256, :]).astype(BF16)
            for k in range(4):
                rows = slice((k % 2) * 256 + n * 64, (k % 2) * 256 + n * 64 + 64)
                xs[k // 2, rows, part * SPAN : part * SPAN + SPAN] = block[k * 64 : k * 64 + 64]
    for b, padded in enumerate((padded0, padded1)):
        turned = lax.dot_general(spread, xs[b], (((1,), (1,)), ((), ())), preferred_element_type=F32)
        power = jnp.sum(turned * turned, axis=0, keepdims=True) * (1.0 / TIME)
        band[b : b + 1, :] = power[:, :256] + power[:, 256:]
        spectra = dot(turned.astype(BF16), dftv[...])
        before = pltpu.roll(spectra[168:], 1, 0)
        padded[0:88, :] = jnp.where(iota(0, (88, 512)) % 8 == 0, 0.0, before)
        padded[88:344, :] = spectra
    results = []
    for b, (padded, even, odd) in enumerate(((padded0, even0, odd0), (padded1, even1, odd1))):
        for n in range(4):
            lanes = slice(n * 128, n * 128 + 128)
            series = protov[0:1, lanes] * padded[88:344, lanes]
            for tap in range(1, TAPS):
                series = series + protov[tap : tap + 1, lanes] * padded[88 - 8 * tap : 344 - 8 * tap, lanes]
            after = pltpu.roll(series[:32], 31, 0)
            after = jnp.where(iota(0, (32, 128)) % 8 == 7, 0.0, after)
            even[0:256, lanes] = series.astype(BF16)
            even[256:288, lanes] = after.astype(BF16)
            odd[0:272, lanes] = jnp.concatenate([series[8:], after[:24]], axis=0).astype(BF16)
        shifted = [even[0:256], odd[0:256], even[16:272], odd[16:272], even[32:288]]
        lhs = jnp.concatenate(
            [jnp.concatenate([block[:, p * 256 : p * 256 + 256] for block in shifted], axis=1) for p in range(2)], axis=0
        )
        product = dot(lhs, tv[b])
        real = product[:256, :256] + product[256:, 256:]
        imag = product[256:, :256] - product[:256, 256:]
        results.append(jnp.concatenate([real, imag], axis=1).astype(BF16))
    final = ones_where(col == (row % 4) * 64 + ((row // 4) % 8) * 8 + row // 32)
    for j in range(4):
        rows = slice(64 * j, 64 * j + 64)
        block = jnp.concatenate(
            [
                jnp.concatenate([results[b][rows, half * 128 + q * 256 : half * 128 + q * 256 + 128] for q in range(2)], axis=1)
                for half in range(2) for b in range(2)
            ],
            axis=0,
        )
        block = dot(final, block).astype(BF16)
        for q in range(2):
            for k in range(8):
                out[q, 128 * k + 32 * j : 128 * k + 32 * j + 32, :] = block[32 * k : 32 * k + 32, q * 128 : q * 128 + 128]


def in_hbm(array):
    return pltpu.with_memory_space_constraint(array, pltpu.HBM)


def on_device(voltages, weights, flags, dm_index):
    hbm = pl.BlockSpec(memory_space=pl.ANY)
    vmem = pl.BlockSpec(memory_space=pltpu.VMEM)
    dma = pltpu.SemaphoreType.DMA
    params = dict(vmem_limit_bytes=24 * 1024 * 1024)
    beams, tables, dft, proto = pl.pallas_call(
        body,
        out_shape=(
            jax.ShapeDtypeStruct((PARTS, 64, 2, 8, SPAN), BF16),
            jax.ShapeDtypeStruct((2, NBLOCK * CHANNELS, 512), BF16),
            jax.ShapeDtypeStruct((512, 512), BF16),
            jax.ShapeDtypeStruct((TAPS, 512), F32),
        ),
        in_specs=[hbm] * 7,
        out_specs=(vmem,) * 4,
        scratch_shapes=[
            pltpu.VMEM((16, 4, 2, 2, 16, 256), BF16),
            pltpu.VMEM((PARTS, 64, 4, 8, SPAN), BF16),
            pltpu.VMEM((PARTS, 64, 2, 4, 8, SPAN), BF16),
            pltpu.VMEM((PARTS, 64, 2, 4, 8, SPAN), BF16),
            pltpu.VMEM((2, 2, 256, 1024), BF16),
            pltpu.VMEM((DMS, 16, 512), F32),
            pltpu.VMEM((1, 64), jnp.int32),
            pltpu.SMEM((2,), jnp.int32),
            pltpu.VMEM((2, 256, 2 * SPAN), BF16),
            pltpu.VMEM((PARTS, 64, 8, SPAN), BF16),
            pltpu.VMEM((PARTS, 64, 2, 8, SPAN), BF16),
            pltpu.VMEM((16, 256), F32),
            dma((8,)),
            pltpu.SemaphoreType.REGULAR,
            dma,
            dma,
            *[dma((PARTS,)) for _ in range(6)],
        ],
        compiler_params=pltpu.CompilerParams(collective_id=0, has_side_effects=True, **params),
        name="beamform",
    )(
        in_hbm(voltages.reshape(16, 4, 2, 2, 16, TIME)),
        in_hbm(weights),
        in_hbm(flags),
        in_hbm(dm_index),
        in_hbm(jnp.asarray(chirp_rows()).astype(BF16).astype(F32)),
        in_hbm(jnp.asarray(dft_rows()).astype(BF16)),
        in_hbm(jnp.asarray(prototype())),
    )
    dedispersed, bandpass = pl.pallas_call(
        tail,
        out_shape=(
            jax.ShapeDtypeStruct((2, 2 * TIME * 2, 128), BF16),
            jax.ShapeDtypeStruct((2, CHANNELS), F32),
        ),
        in_specs=[vmem] * 4,
        out_specs=(vmem, vmem),
        scratch_shapes=[
            pltpu.VMEM((2, 512, 256), BF16),
            *[pltpu.VMEM((344, 512), F32) for _ in range(2)],
            *[pltpu.VMEM((288, 512), BF16) for _ in range(2)],
            *[pltpu.VMEM((272, 512), BF16) for _ in range(2)],
        ],
        compiler_params=pltpu.CompilerParams(**params),
        name="synthesis",
    )(
        beams.reshape(PARTS, 1024, SPAN),
        tables,
        dft,
        proto,
    )
    dedispersed = dedispersed.reshape(2, 512, 2, 128).transpose(0, 2, 1, 3).reshape(2, 2, TIME * CHANNELS)
    return dedispersed, bandpass


def solution(mesh):
    return jax.shard_map(
        on_device,
        mesh=mesh,
        in_specs=(
            P(None, ("stn", "chan"), None, None),
            P(None, ("stn", "chan"), None, None),
            P(("stn", "chan"), None),
            P(("stn", "chan")),
        ),
        out_specs=(P(None, ("stn", "chan"), None), P(("stn", "chan"), None)),
        check_vma=False,
    )
```

time: 54.6 us -> 53.1 us (0.973)
  Pallas kernels: 53.9 us -> 52.3 us
    pallas_call x1, Pallas kernels: 5.72 us -> 4.3 us  [on_device(): pl.pallas_call(tail, out_shape=(jax.ShapeDtypeStruct((2, 2 * TIME * 2, 12...]
where the time goes in v2:
time: 53.1 us; the launch traced here: 53 us
  Pallas kernels  52.3 us (98%)
  between operations  0.64 us (1%)
    pallas_call x1, Pallas kernels, on_device(): pl.pallas_call(body, out_shape=(jax.ShapeDtypeStruct((PARTS, 64, 2, 8, SP...  48 us
    pallas_call x1, Pallas kernels, on_device(): pl.pallas_call(tail, out_shape=(jax.ShapeDtypeStruct((2, 2 * TIME * 2, 12...  4.3 us

profile of v2, /device:TPU:1, one launch (start us, length us, event | category | flops | bytes accessed | tf_op | source)
XLA Modules:
  0.0 53.0 jit_solution(9205172022091085364)
XLA Ops:
  0.6 48.0 %beamform.1 = (bf16[2,64,2,8,128]{4,3,2,1,0:T(8,128)(2,1)S(1)}, bf16[2,1280,512]{2,1,0:T(8,128)(2,1)S(1)}, bf16[512,512]{1,0:T(8,128)(2,1)S(1)}, f32[12,512]{1,0:T(8,128)S(1)}) custom-call(bf16[16,4,2,2,16,256]{5,4,3,2,1,0:T(8,128)(2,1)} %bitcast.8, bf16[2,2,256,1024]{3,2,1,0:T(8,128)(2,1)} %wgt.1, s32[1,64]{1,0:T(1,128)} %flags.1, s32[2]{0:T(128)} %dm.1, ...), custom_call_target="tpu_custom_call" | custom-call | tf_op jit(solution)/shard_map/beamform/pallas_call | solution.py:304
  48.7 4.3 %synthesis.1 = (bf16[2,1024,128]{2,1,0:T(8,128)(2,1)}, f32[2,256]{1,0:T(2,128)}) custom-call(bf16[2,1024,128]{2,1,0:T(8,128)(2,1)S(1)} %bitcast.7, bf16[2,1280,512]{2,1,0:T(8,128)(2,1)S(1)} %get-tuple-element.9.tv, bf16[512,512]{1,0:T(8,128)(2,1)S(1)} %get-tuple-element.10.dftv, f32[12,512]{1,0:T(8,128)S(1)} %get-tuple-element.11.protov), custom_call_target="tpu_custom_call" | custom-call | tf_op jit(solution)/shard_map/synthesis/pallas_call | solution.py:344

commit v3 on v2

--- a/solution.py
+++ b/solution.py
@@ -84,7 +84,7 @@
 def body(
     volt, wgt, flags, dm, chirps, dft, proto, recv2, tables, dftv, protov,
     vin, give, send, recv, win, chv, flagv, dmv, beams, give2, send2, keep,
-    load_sem, plane_sem, given, given2, sent, sent2, sibling_sem, sibling_sem2, recv_sem, recv_sem2,
+    load_sem, plane_sem, given, given2, sent, sent2, sibling_sem, sibling_sem2, recv_sem, recv_sem2, pack_sem, packs_sent, relays_sent, *stages,
 ):
     x = lax.rem(lax.axis_index("chan"), 4)
     y = lax.axis_index("chan") // 4
@@ -111,13 +111,13 @@
     line = [(zs[dz] * 2 + core, ys[0] + x) for dz in range(1, 4)]
     plane = [(z * 2 + core, ys[dy] + xs[dx]) for dy in range(4) for dx in range(4) if (dy, dx) != (0, 0)]
     greeted = [sibling] + line + plane
-    for place in greeted:
-        pl.semaphore_signal(barrier, inc=1, device_id=place, device_id_type=MESH)
+    for peer in greeted:
+        pl.semaphore_signal(barrier, inc=1, device_id=peer, device_id_type=MESH)
 
     def hand_over(part, give, send, given, sibling_sem):
         pltpu.make_async_remote_copy(
             src_ref=give.at[part],
-            dst_ref=send.at[part, :, core],
+            dst_ref=send.at[part, :, :, :, core] if len(send.shape) == 8 else send.at[part, :, core],
             send_sem=given,
             recv_sem=sibling_sem.at[part],
             device_id=sibling,
@@ -140,6 +140,68 @@
                     device_id_type=MESH,
                 ).start()
 
+    by_z, by_x, by_y, by_xz, by_yz, by_xy, by_xyz = stages
+
+    def place(steps):
+        dz, dy, dx = steps
+        return zs[dz % 4] * 2 + core, ys[dy % 4] + xs[dx % 4]
+
+    def packs(part):
+        near = (-1, 0, 1)
+        listed = []
+        for m in range(3):
+            listed.append(((3, m, slice(0, 3)), by_z.at[part, m], (1, 0, 0), [(1, m - 1, d) for d in near]))
+            listed.append(((m, slice(0, 3), 3), by_x.at[part, m], (0, 0, 1), [(m - 1, d, 1) for d in near]))
+            listed.append(((m, 3, slice(0, 3)), by_y.at[part, m], (0, 1, 0), [(m - 1, 1, d) for d in near]))
+        listed.append(((3, slice(0, 3), 3), by_xz.at[part], (1, 0, 1), [(1, d, 1) for d in near]))
+        listed.append(((3, 3, slice(0, 3)), by_yz.at[part], (1, 1, 0), [(1, 1, d) for d in near]))
+        for m in range(3):
+            listed.append(((m, 3, 3), by_xy.at[part, m], (0, 1, 1), [(m - 1, 1, 1)]))
+        listed.append(((3, 3, 3), by_xyz.at[part], (1, 1, 1), [(1, 1, 1)]))
+        return [(15 * part + n, *pack) for n, pack in enumerate(listed)]
+
+    def send_packs(part):
+        share = send.at[part, :, :, :, 1 - core]
+        pltpu.make_async_copy(share, share, sibling_sem.at[part]).wait()
+        for n, at, stage, steps, _ in packs(part):
+            pltpu.make_async_remote_copy(
+                src_ref=send.at[part, at[0], at[1], at[2]],
+                dst_ref=stage,
+                send_sem=packs_sent,
+                recv_sem=pack_sem.at[n],
+                device_id=place(steps),
+                device_id_type=MESH,
+            ).start()
+
+    def send_direct(part):
+        pltpu.make_async_copy(send.at[part, 1, 1, 1], recv.at[part, chip], recv_sem.at[part]).start()
+        for steps in exchange_order():
+            if 2 not in steps and steps != (0, 0, 0):
+                at = [(d + 1) % 4 for d in steps]
+                pltpu.make_async_remote_copy(
+                    src_ref=send.at[part, at[0], at[1], at[2]],
+                    dst_ref=recv.at[part, chip],
+                    send_sem=sent.at[part],
+                    recv_sem=recv_sem.at[part],
+                    device_id=place(steps),
+                    device_id_type=MESH,
+                ).start()
+
+    def relay_packs(part):
+        for n, _, stage, steps, onward in packs(part):
+            pltpu.make_async_copy(stage, stage, pack_sem.at[n]).wait()
+            dz, dy, dx = (-d % 4 for d in steps)
+            origin = zs[dz] * CHAN_AXIS + ys[dy] + xs[dx]
+            for m, further in enumerate(onward):
+                pltpu.make_async_remote_copy(
+                    src_ref=stage.at[m] if len(onward) > 1 else stage,
+                    dst_ref=recv.at[part, origin],
+                    send_sem=relays_sent,
+                    recv_sem=recv_sem.at[part],
+                    device_id=place(further),
+                    device_id_type=MESH,
+                ).start()
+
     flag_load.wait()
     row, col = iota(0), iota(1)
     hits = ones_where(iota(0, (256, 64)) == flagv[...])
@@ -147,29 +209,33 @@
     keep_rows = ones_where((count < 0.5) & (row % 16 == col % 16))
     keep[...] = dot(ones_where(iota(1, (16, 256)) // 16 == iota(0, (16, 256))), keep_rows)
 
-    there = (row // 32) * 2 + (row // 8) % 2
-    swap = jnp.where((col // 16 == ((row // 16) % 2) * 8 + row % 8) & (col % 16 == there), 1.0, 0.0)
-
     def sort_out(number):
+        way = 1 + 2 * number
+        there = (row // 128) * 8 + ((x + (row // 32 + 3) % 4 * way) % 4) * 2 + (row // 8) % 2
+        swap = jnp.where((col // 16 == ((row // 16) % 2) * 8 + row % 8) & (col % 16 == there), 1.0, 0.0)
         for zz in range(4):
             for half in range(2):
                 block = vin[:, zz, number, half].reshape(256, 256)
                 mine = (swap * keep[pl.ds((zz * 2 + number) * 2 + half, 1), :]).astype(BF16)
-                yield slice(zz * 16 + half * 8, zz * 16 + half * 8 + 8), dot(mine, block).astype(BF16).reshape(8, 4, 8, 256)
+                sorted_block = dot(mine, block).astype(BF16)
+                for one in range(2):
+                    mz = lax.rem((zz + 4 - z) * way + 1, 4)
+                    my = lax.rem((half * 2 + one + 4 - y) * way + 1, 4)
+                    yield mz, my, sorted_block[one * 128 : one * 128 + 128].reshape(4, 4, 8, 256)
 
     volt_loads[0].wait()
-    for chips, block in sort_out(1 - core):
+    for mz, my, block in sort_out(1 - core):
         for part in range(PARTS):
-            give[part, chips] = block[..., part * SPAN : part * SPAN + SPAN]
+            give[part, mz, my] = block[..., part * SPAN : part * SPAN + SPAN]
     pl.semaphore_wait(barrier, len(greeted))
-    for place in line:
-        pl.semaphore_signal(plane_sem, inc=1, device_id=place, device_id_type=MESH)
+    for peer in line:
+        pl.semaphore_signal(plane_sem, inc=1, device_id=peer, device_id_type=MESH)
     for part in range(PARTS):
         hand_over(part, give, send, given, sibling_sem)
     volt_loads[1].wait()
-    for chips, block in sort_out(core):
+    for mz, my, block in sort_out(core):
         for part in range(PARTS):
-            send[part, chips, core] = block[..., part * SPAN : part * SPAN + SPAN]
+            send[part, mz, my, :, core] = block[..., part * SPAN : part * SPAN + SPAN]
     loads = [
         pltpu.make_async_copy(source, target, load_sem.at[n])
         for n, (source, target) in enumerate(
@@ -179,8 +245,12 @@
     for load in loads:
         load.start()
     pl.semaphore_wait(plane_sem, len(line))
-    for part in range(PARTS):
-        exchange(part, send, recv.at[part, chip], sibling_sem, sent, recv_sem)
+    send_packs(0)
+    send_direct(0)
+    send_packs(1)
+    relay_packs(0)
+    send_direct(1)
+    relay_packs(1)
     for load in loads:
         load.wait()
 
@@ -233,8 +303,12 @@
 
     for blocks, sem in ((give, given), (give2, given2)):
         pltpu.make_async_copy(blocks, blocks, sem).wait()
+    for sem in (packs_sent, relays_sent):
+        for part in range(PARTS):
+            blocks = recv.at[part, 0:37]
+            pltpu.make_async_copy(blocks, blocks, sem).wait()
     for part in range(PARTS):
-        for blocks, sem in ((send.at[part, 0:63], sent), (send2.at[part, 0:63], sent2), (recv2.at[part], recv_sem2)):
+        for blocks, sem in ((recv.at[part, 0:26], sent), (send2.at[part, 0:63], sent2), (recv2.at[part], recv_sem2)):
             pltpu.make_async_copy(blocks, blocks, sem.at[part]).wait()
 
 
@@ -313,8 +387,8 @@
         out_specs=(vmem,) * 4,
         scratch_shapes=[
             pltpu.VMEM((16, 4, 2, 2, 16, 256), BF16),
-            pltpu.VMEM((PARTS, 64, 4, 8, SPAN), BF16),
-            pltpu.VMEM((PARTS, 64, 2, 4, 8, SPAN), BF16),
+            pltpu.VMEM((PARTS, 4, 4, 4, 4, 8, SPAN), BF16),
+            pltpu.VMEM((PARTS, 4, 4, 4, 2, 4, 8, SPAN), BF16),
             pltpu.VMEM((PARTS, 64, 2, 4, 8, SPAN), BF16),
             pltpu.VMEM((2, 2, 256, 1024), BF16),
             pltpu.VMEM((DMS, 16, 512), F32),
@@ -329,6 +403,13 @@
             dma,
             dma,
             *[dma((PARTS,)) for _ in range(6)],
+            dma((30,)),
+            dma,
+            dma,
+            *[
+                pltpu.VMEM((PARTS,) + shape + (2, 4, 8, SPAN), BF16)
+                for shape in [(3, 3), (3, 3), (3, 3), (3,), (3,), (3,), ()]
+            ],
         ],
         compiler_params=pltpu.CompilerParams(collective_id=0, has_side_effects=True, **params),
         name="beamform",

time: 53.1 us -> 51 us (0.960)
  Pallas kernels: 52.3 us -> 50.2 us
    pallas_call x1, Pallas kernels: 48 us -> 45.9 us  [on_device(): pl.pallas_call(body, out_shape=(jax.ShapeDtypeStruct((PARTS, 64, 2, 8, SP...]
where the time goes in v3:
time: 51 us; the launch traced here: 50.8 us
  Pallas kernels  50.2 us (98%)
  between operations  0.64 us (1%)
    pallas_call x1, Pallas kernels, on_device(): pl.pallas_call(body, out_shape=(jax.ShapeDtypeStruct((PARTS, 64, 2, 8, SP...  45.9 us
    pallas_call x1, Pallas kernels, on_device(): pl.pallas_call(tail, out_shape=(jax.ShapeDtypeStruct((2, 2 * TIME * 2, 12...  4.29 us

profile of v3, /device:TPU:1, one launch (start us, length us, event | category | flops | bytes accessed | tf_op | source)
XLA Modules:
  0.0 50.8 jit_solution(7357285199489278376)
XLA Ops:
  0.6 45.9 %beamform.1 = (bf16[2,64,2,8,128]{4,3,2,1,0:T(8,128)(2,1)S(1)}, bf16[2,1280,512]{2,1,0:T(8,128)(2,1)S(1)}, bf16[512,512]{1,0:T(8,128)(2,1)S(1)}, f32[12,512]{1,0:T(8,128)S(1)}) custom-call(bf16[16,4,2,2,16,256]{5,4,3,2,1,0:T(8,128)(2,1)} %bitcast.8, bf16[2,2,256,1024]{3,2,1,0:T(8,128)(2,1)} %wgt.1, s32[1,64]{1,0:T(1,128)} %flags.1, s32[2]{0:T(128)} %dm.1, ...), custom_call_target="tpu_custom_call" | custom-call | tf_op jit(solution)/shard_map/beamform/pallas_call | solution.py:378
  46.5 4.3 %synthesis.1 = (bf16[2,1024,128]{2,1,0:T(8,128)(2,1)}, f32[2,256]{1,0:T(2,128)}) custom-call(bf16[2,1024,128]{2,1,0:T(8,128)(2,1)S(1)} %bitcast.7, bf16[2,1280,512]{2,1,0:T(8,128)(2,1)S(1)} %get-tuple-element.9.tv, bf16[512,512]{1,0:T(8,128)(2,1)S(1)} %get-tuple-element.10.dftv, f32[12,512]{1,0:T(8,128)S(1)} %get-tuple-element.11.protov), custom_call_target="tpu_custom_call" | custom-call | tf_op jit(solution)/shard_map/synthesis/pallas_call | solution.py:425

commit v4 on v3

--- a/solution.py
+++ b/solution.py
@@ -82,8 +82,8 @@
 
 
 def body(
-    volt, wgt, flags, dm, chirps, dft, proto, recv2, tables, dftv, protov,
-    vin, give, send, recv, win, chv, flagv, dmv, beams, give2, send2, keep,
+    volt, wgt, flags, dm, chirps, dft, proto, recv2, tables, dftv, protov, series0, last0, power0,
+    vin, give, send, recv, win, chv, flagv, dmv, beams, give2, send2, keep, ordered, padded,
     load_sem, plane_sem, given, given2, sent, sent2, sibling_sem, sibling_sem2, recv_sem, recv_sem2, pack_sem, packs_sent, relays_sent, *stages,
 ):
     x = lax.rem(lax.axis_index("chan"), 4)
@@ -301,6 +301,18 @@
         hand_over(part, give2, send2, given2, sibling_sem2)
         exchange(part, send2, recv2.at[part, chip], sibling_sem2, sent2, recv_sem2)
 
+    arrived = recv2.at[0]
+    pltpu.make_async_copy(arrived, arrived, recv_sem2.at[0]).wait()
+    for b, power, last in front(
+        lambda n: recv2[0, n * 16 : n * 16 + 16].reshape(256, SPAN), lambda b: 0.0, dftv, protov, ordered, padded
+    ):
+        power0[b : b + 1, :] = power
+        last0[b] = last
+    for b in range(2):
+        for n in range(4):
+            lanes, series = synthesise(b, n, protov, padded)
+            series0[b, :, lanes] = series
+
     for blocks, sem in ((give, given), (give2, given2)):
         pltpu.make_async_copy(blocks, blocks, sem).wait()
     for sem in (packs_sent, relays_sent):
@@ -308,62 +320,98 @@
             blocks = recv.at[part, 0:37]
             pltpu.make_async_copy(blocks, blocks, sem).wait()
     for part in range(PARTS):
-        for blocks, sem in ((recv.at[part, 0:26], sent), (send2.at[part, 0:63], sent2), (recv2.at[part], recv_sem2)):
+        for blocks, sem in ((recv.at[part, 0:26], sent), (send2.at[part, 0:63], sent2)):
             pltpu.make_async_copy(blocks, blocks, sem.at[part]).wait()
-
-
-def tail(xv, tv, dftv, protov, out, band, xs, padded0, padded1, even0, even1, odd0, odd1):
+    arrived = recv2.at[1]
+    pltpu.make_async_copy(arrived, arrived, recv_sem2.at[1]).wait()
+
+
+def front(chunk, before_first, dftv, protov, xs, padded):
     row, col = iota(0), iota(1)
     sort = ones_where(col == ((row % 32) // 2 * 2 + (row % 64) // 32) * 8 + (row // 64) * 2 + row % 2)
-    spread = ones_where(col == (row % 8) * 32 + row // 8)
-    for part in range(PARTS):
+    spread = ones_where(iota(1, (SPAN, SPAN)) == (iota(0, (SPAN, SPAN)) % 8) * 16 + iota(0, (SPAN, SPAN)) // 8)
+    for n in range(4):
+        block = dot(sort, chunk(n)).astype(BF16)
+        for k in range(4):
+            xs[k // 2, (k % 2) * 256 + n * 64 : (k % 2) * 256 + n * 64 + 64, :] = block[k * 64 : k * 64 + 64]
+    for b in range(2):
+        turned = lax.dot_general(spread, xs[b], (((1,), (1,)), ((), ())), preferred_element_type=F32)
+        power = jnp.sum(turned * turned, axis=0, keepdims=True)
+        spectra = dot(turned.astype(BF16), dftv[...])
+        last = spectra[SPAN - 88 :]
+        first = iota(0, (88, 512)) % 8 == 0
+        padded[b, 0:88, :] = jnp.where(first, before_first(b), pltpu.roll(last, 1, 0))
+        padded[b, 88 : 88 + SPAN, :] = spectra
+        yield b, power, pltpu.roll(last, 81, 0)
+
+
+def synthesise(b, n, protov, padded):
+    lanes = slice(n * 128, n * 128 + 128)
+    series = protov[0:1, lanes] * padded[b, 88 : 88 + SPAN, lanes]
+    for tap in range(1, TAPS):
+        series = series + protov[tap : tap + 1, lanes] * padded[b, 88 - 8 * tap : 88 - 8 * tap + SPAN, lanes]
+    return lanes, series
+
+
+def tail(
+    xv, tv, dftv, protov, series0, last0, power0, out, band,
+    xs, padded, even00, even01, even10, even11, odd00, odd01, odd10, odd11, outv, bandv, out_sem,
+):
+    band_copy = pltpu.make_async_copy(bandv, band, out_sem.at[2])
+    for b, power, _ in front(lambda n: xv[1, n * 256 : n * 256 + 256, :], lambda b: last0[b], dftv, protov, xs, padded):
+        power = (power + power0[b : b + 1, :]) * (1.0 / TIME)
+        bandv[b : b + 1, :] = power[:, :256] + power[:, 256:]
+    band_copy.start()
+    results = []
+    final_lane = iota(0, (32, 128)) % 8 == 7
+    for b, evens, odds in ((0, (even00, even01), (odd00, odd01)), (1, (even10, even11), (odd10, odd11))):
         for n in range(4):
-            block = dot(sort, xv[part, n * 256 : n * 256 + 256, :]).astype(BF16)
-            for k in range(4):
-                rows = slice((k % 2) * 256 + n * 64, (k % 2) * 256 + n * 64 + 64)
-                xs[k // 2, rows, part * SPAN : part * SPAN + SPAN] = block[k * 64 : k * 64 + 64]
-    for b, padded in enumerate((padded0, padded1)):
-        turned = lax.dot_general(spread, xs[b], (((1,), (1,)), ((), ())), preferred_element_type=F32)
-        power = jnp.sum(turned * turned, axis=0, keepdims=True) * (1.0 / TIME)
-        band[b : b + 1, :] = power[:, :256] + power[:, 256:]
-        spectra = dot(turned.astype(BF16), dftv[...])
-        before = pltpu.roll(spectra[168:], 1, 0)
-        padded[0:88, :] = jnp.where(iota(0, (88, 512)) % 8 == 0, 0.0, before)
-        padded[88:344, :] = spectra
-    results = []
-    for b, (padded, even, odd) in enumerate(((padded0, even0, odd0), (padded1, even1, odd1))):
-        for n in range(4):
-            lanes = slice(n * 128, n * 128 + 128)
-            series = protov[0:1, lanes] * padded[88:344, lanes]
-            for tap in range(1, TAPS):
-                series = series + protov[tap : tap + 1, lanes] * padded[88 - 8 * tap : 344 - 8 * tap, lanes]
-            after = pltpu.roll(series[:32], 31, 0)
-            after = jnp.where(iota(0, (32, 128)) % 8 == 7, 0.0, after)
-            even[0:256, lanes] = series.astype(BF16)
-            even[256:288, lanes] = after.astype(BF16)
-            odd[0:272, lanes] = jnp.concatenate([series[8:], after[:24]], axis=0).astype(BF16)
-        shifted = [even[0:256], odd[0:256], even[16:272], odd[16:272], even[32:288]]
+            lanes, series1 = synthesise(b, n, protov, padded)
+            both = (series0[b, :, lanes], series1)
+            following = (pltpu.roll(series1[:32], 7, 0), 0.0)
+            for series, follow, even, odd in zip(both, following, evens, odds):
+                after = jnp.where(final_lane, follow, pltpu.roll(series[:32], 31, 0))
+                even[0:SPAN, lanes] = series.astype(BF16)
+                even[SPAN : SPAN + 32, lanes] = after.astype(BF16)
+                odd[0 : SPAN + 16, lanes] = jnp.concatenate([series[8:], after[:24]], axis=0).astype(BF16)
+        shifted = [
+            [even[0:SPAN], odd[0:SPAN], even[16 : 16 + SPAN], odd[16 : 16 + SPAN], even[32 : 32 + SPAN]]
+            for even, odd in zip(evens, odds)
+        ]
         lhs = jnp.concatenate(
-            [jnp.concatenate([block[:, p * 256 : p * 256 + 256] for block in shifted], axis=1) for p in range(2)], axis=0
+            [
+                jnp.concatenate([block[:, p * 256 : p * 256 + 256] for block in blocks], axis=1)
+                for p in range(2) for blocks in shifted
+            ],
+            axis=0,
         )
         product = dot(lhs, tv[b])
         real = product[:256, :256] + product[256:, 256:]
         imag = product[256:, :256] - product[:256, 256:]
         results.append(jnp.concatenate([real, imag], axis=1).astype(BF16))
+    row, col = iota(0), iota(1)
     final = ones_where(col == (row % 4) * 64 + ((row // 4) % 8) * 8 + row // 32)
-    for j in range(4):
-        rows = slice(64 * j, 64 * j + 64)
-        block = jnp.concatenate(
-            [
-                jnp.concatenate([results[b][rows, half * 128 + q * 256 : half * 128 + q * 256 + 128] for q in range(2)], axis=1)
-                for half in range(2) for b in range(2)
-            ],
-            axis=0,
-        )
-        block = dot(final, block).astype(BF16)
-        for q in range(2):
-            for k in range(8):
-                out[q, 128 * k + 32 * j : 128 * k + 32 * j + 32, :] = block[32 * k : 32 * k + 32, q * 128 : q * 128 + 128]
+    copies = []
+    for h in range(2):
+        for j in range(2):
+            rows = slice(128 * h + 64 * j, 128 * h + 64 * j + 64)
+            block = jnp.concatenate(
+                [
+                    jnp.concatenate([results[b][rows, half * 128 + q * 256 : half * 128 + q * 256 + 128] for q in range(2)], axis=1)
+                    for half in range(2) for b in range(2)
+                ],
+                axis=0,
+            )
+            block = dot(final, block).astype(BF16)
+            for q in range(2):
+                for k in range(8):
+                    start = 512 * h + 64 * k + 32 * j
+                    outv[q, start : start + 32, :] = block[32 * k : 32 * k + 32, q * 128 : q * 128 + 128]
+        done = pl.ds(512 * h, 512)
+        copies.append(pltpu.make_async_copy(outv.at[:, done], out.at[:, done], out_sem.at[h]))
+        copies[-1].start()
+    for copy in copies + [band_copy]:
+        copy.wait()
 
 
 def in_hbm(array):
@@ -375,16 +423,19 @@
     vmem = pl.BlockSpec(memory_space=pltpu.VMEM)
     dma = pltpu.SemaphoreType.DMA
     params = dict(vmem_limit_bytes=24 * 1024 * 1024)
-    beams, tables, dft, proto = pl.pallas_call(
+    beams, tables, dft, proto, series0, last0, power0 = pl.pallas_call(
         body,
         out_shape=(
             jax.ShapeDtypeStruct((PARTS, 64, 2, 8, SPAN), BF16),
             jax.ShapeDtypeStruct((2, NBLOCK * CHANNELS, 512), BF16),
             jax.ShapeDtypeStruct((512, 512), BF16),
             jax.ShapeDtypeStruct((TAPS, 512), F32),
+            jax.ShapeDtypeStruct((2, SPAN, 512), F32),
+            jax.ShapeDtypeStruct((2, 88, 512), F32),
+            jax.ShapeDtypeStruct((2, 512), F32),
         ),
         in_specs=[hbm] * 7,
-        out_specs=(vmem,) * 4,
+        out_specs=(vmem,) * 7,
         scratch_shapes=[
             pltpu.VMEM((16, 4, 2, 2, 16, 256), BF16),
             pltpu.VMEM((PARTS, 4, 4, 4, 4, 8, SPAN), BF16),
@@ -398,6 +449,8 @@
             pltpu.VMEM((PARTS, 64, 8, SPAN), BF16),
             pltpu.VMEM((PARTS, 64, 2, 8, SPAN), BF16),
             pltpu.VMEM((16, 256), F32),
+            pltpu.VMEM((2, 512, SPAN), BF16),
+            pltpu.VMEM((2, 88 + SPAN, 512), F32),
             dma((8,)),
             pltpu.SemaphoreType.REGULAR,
             dma,
@@ -428,13 +481,16 @@
             jax.ShapeDtypeStruct((2, 2 * TIME * 2, 128), BF16),
             jax.ShapeDtypeStruct((2, CHANNELS), F32),
         ),
-        in_specs=[vmem] * 4,
-        out_specs=(vmem, vmem),
+        in_specs=[vmem] * 7,
+        out_specs=(hbm, hbm),
         scratch_shapes=[
-            pltpu.VMEM((2, 512, 256), BF16),
-            *[pltpu.VMEM((344, 512), F32) for _ in range(2)],
-            *[pltpu.VMEM((288, 512), BF16) for _ in range(2)],
-            *[pltpu.VMEM((272, 512), BF16) for _ in range(2)],
+            pltpu.VMEM((2, 512, SPAN), BF16),
+            pltpu.VMEM((2, 88 + SPAN, 512), F32),
+            *[pltpu.VMEM((SPAN + 32, 512), BF16) for _ in range(4)],
+            *[pltpu.VMEM((SPAN + 16, 512), BF16) for _ in range(4)],
+            pltpu.VMEM((2, 2 * TIME * 2, 128), BF16),
+            pltpu.VMEM((2, CHANNELS), F32),
+            dma((3,)),
         ],
         compiler_params=pltpu.CompilerParams(**params),
         name="synthesis",
@@ -443,6 +499,9 @@
         tables,
         dft,
         proto,
+        series0,
+        last0,
+        power0,
     )
     dedispersed = dedispersed.reshape(2, 512, 2, 128).transpose(0, 2, 1, 3).reshape(2, 2, TIME * CHANNELS)
     return dedispersed, bandpass

time: 51 us -> 50.4 us (0.988)
  Pallas kernels: 50.2 us -> 49.6 us
    pallas_call x1, Pallas kernels: 4.29 us -> 3.69 us  [on_device(): pl.pallas_call(tail, out_shape=(jax.ShapeDtypeStruct((2, 2 * TIME * 2, 12...]
where the time goes in v4:
time: 50.4 us; the launch traced here: 50.2 us
  Pallas kernels  49.6 us (98%)
  between operations  0.64 us (1%)
    pallas_call x1, Pallas kernels, on_device(): pl.pallas_call(body, out_shape=(jax.ShapeDtypeStruct((PARTS, 64, 2, 8, SP...  45.9 us
    pallas_call x1, Pallas kernels, on_device(): pl.pallas_call(tail, out_shape=(jax.ShapeDtypeStruct((2, 2 * TIME * 2, 12...  3.69 us

profile of v4, /device:TPU:1, one launch (start us, length us, event | category | flops | bytes accessed | tf_op | source)
XLA Modules:
  0.0 50.2 jit_solution(8118966925841958403)
XLA Ops:
  0.6 45.9 %beamform.1 = (bf16[2,64,2,8,128]{4,3,2,1,0:T(8,128)(2,1)S(1)}, bf16[2,1280,512]{2,1,0:T(8,128)(2,1)S(1)}, bf16[512,512]{1,0:T(8,128)(2,1)S(1)}, f32[12,512]{1,0...) custom-call(bf16[16,4,2,2,16,256]{5,4,3,2,1,0:T(8,128)(2,1)} %bitcast.8, ...), custom_call_target="tpu_custom_call" | custom-call | tf_op jit(solution)/shard_map/beamform/pallas_call | solution.py:426
  46.5 3.7 %synthesis.1 = (bf16[2,1024,128]{2,1,0:T(8,128)(2,1)}, f32[2,256]{1,0:T(2,128)}) custom-call(bf16[2,1024,128]{2,1,0:T(8,128)(2,1)S(1)} %bitcast.7, bf16[2,1280,512]{2,1,0:T(8,128)(2,1)S(1)} %get-tuple-element.12.tv, bf16[512,512]{1,0:T(8,128)(2,1)S(1)} %get-tuple-element.13.dftv, f32[12,512]{1,0:T(8,128)S(1)} %get-tuple-element.14.protov, ...), custom_call_target="tpu_custom_call" | custom-call | tf_op jit(solution)/shard_map/synthesis/pallas_call | solution.py:478

commit v5 on v4

--- a/solution.py
+++ b/solution.py
@@ -83,7 +83,7 @@
 
 def body(
     volt, wgt, flags, dm, chirps, dft, proto, recv2, tables, dftv, protov, series0, last0, power0,
-    vin, give, send, recv, win, chv, flagv, dmv, beams, give2, send2, keep, ordered, padded,
+    vin, give, send, recv, win, chv, flagv, dmv, beams, give2, send2, keep, ordered, padded, acc,
     load_sem, plane_sem, given, given2, sent, sent2, sibling_sem, sibling_sem2, recv_sem, recv_sem2, pack_sem, packs_sent, relays_sent, *stages,
 ):
     x = lax.rem(lax.axis_index("chan"), 4)
@@ -153,10 +153,9 @@
             listed.append(((3, m, slice(0, 3)), by_z.at[part, m], (1, 0, 0), [(1, m - 1, d) for d in near]))
             listed.append(((m, slice(0, 3), 3), by_x.at[part, m], (0, 0, 1), [(m - 1, d, 1) for d in near]))
             listed.append(((m, 3, slice(0, 3)), by_y.at[part, m], (0, 1, 0), [(m - 1, 1, d) for d in near]))
+            listed.append(((m, 3, 3), by_xy.at[part, m], (0, 1, 1), [(m - 1, 1, 1)]))
         listed.append(((3, slice(0, 3), 3), by_xz.at[part], (1, 0, 1), [(1, d, 1) for d in near]))
         listed.append(((3, 3, slice(0, 3)), by_yz.at[part], (1, 1, 0), [(1, 1, d) for d in near]))
-        for m in range(3):
-            listed.append(((m, 3, 3), by_xy.at[part, m], (0, 1, 1), [(m - 1, 1, 1)]))
         listed.append(((3, 3, 3), by_xyz.at[part], (1, 1, 1), [(1, 1, 1)]))
         return [(15 * part + n, *pack) for n, pack in enumerate(listed)]
 
@@ -174,7 +173,7 @@
             ).start()
 
     def send_direct(part):
-        pltpu.make_async_copy(send.at[part, 1, 1, 1], recv.at[part, chip], recv_sem.at[part]).start()
+        pltpu.make_async_copy(send.at[part, 1, 1, 1], recv.at[part, chip], recv_sem.at[part, 0]).start()
         for steps in exchange_order():
             if 2 not in steps and steps != (0, 0, 0):
                 at = [(d + 1) % 4 for d in steps]
@@ -182,7 +181,7 @@
                     src_ref=send.at[part, at[0], at[1], at[2]],
                     dst_ref=recv.at[part, chip],
                     send_sem=sent.at[part],
-                    recv_sem=recv_sem.at[part],
+                    recv_sem=recv_sem.at[part, steps[0]],
                     device_id=place(steps),
                     device_id_type=MESH,
                 ).start()
@@ -197,7 +196,7 @@
                     src_ref=stage.at[m] if len(onward) > 1 else stage,
                     dst_ref=recv.at[part, origin],
                     send_sem=relays_sent,
-                    recv_sem=recv_sem.at[part],
+                    recv_sem=recv_sem.at[part, (steps[0] + further[0]) % 4],
                     device_id=place(further),
                     device_id_type=MESH,
                 ).start()
@@ -272,26 +271,33 @@
         (col // 128 == row % 2) & ((col // 64) % 2 == (row // 2) % 2) & (col % 64 == to_device * 2 + (row // 4) % 2)
     )
     for part in range(PARTS):
-        arrived = recv.at[part]
-        pltpu.make_async_copy(arrived, arrived, recv_sem.at[part]).wait()
-        for c in range(2):
-            both, real, imag = [], [], []
-            for number in range(2):
-                real.append(recv[part, :, number, c].reshape(512, SPAN))
-                imag.append(recv[part, :, number, 2 + c].reshape(512, SPAN))
-            for p in range(2):
+        for n, dz in enumerate((3, 0, 1, 2)):
+            source = zs[-dz % 4]
+            arrived = recv.at[part, pl.ds(pl.multiple_of(source * 16, 16), 16)]
+            pltpu.make_async_copy(arrived, arrived, recv_sem.at[part, dz]).wait()
+            for c in range(2):
+                real, imag, weight_real, weight_imag = [], [], [], []
                 for number in range(2):
-                    for zz in range(4):
-                        inputs = (zz * 2 + number) * 128
-                        both.append(win[p, c, :, inputs : inputs + 128])
-            parts = jnp.concatenate(
-                [
-                    jnp.concatenate(real + [-half for half in imag], axis=0),
-                    jnp.concatenate(imag + real, axis=0),
-                ],
-                axis=1,
-            )
-            beams[c] = dot(jnp.concatenate(both, axis=1), parts).astype(BF16)
+                    chips = pl.ds(pl.multiple_of(source * 16, 16), 16)
+                    inputs = pl.ds(pl.multiple_of((source * 2 + number) * 128, 128), 128)
+                    real.append(recv[part, chips, number, c].reshape(128, SPAN))
+                    imag.append(recv[part, chips, number, 2 + c].reshape(128, SPAN))
+                    weight_real.append(win[0, c, :, inputs])
+                    weight_imag.append(win[1, c, :, inputs])
+                parts = jnp.concatenate(
+                    [
+                        jnp.concatenate(real + [-half for half in imag], axis=0),
+                        jnp.concatenate(imag + real, axis=0),
+                    ],
+                    axis=1,
+                )
+                product = dot(jnp.concatenate(weight_real + weight_imag, axis=1), parts)
+                if n == 0:
+                    acc[c] = product
+                elif n < 3:
+                    acc[c] += product
+                else:
+                    beams[c] = (acc[c] + product).astype(BF16)
         for zz in range(4):
             rows = slice(zz * 64, zz * 64 + 64)
             block = jnp.concatenate([beams[c, rows, q * SPAN : q * SPAN + SPAN] for c in range(2) for q in range(2)], axis=0)
@@ -451,11 +457,14 @@
             pltpu.VMEM((16, 256), F32),
             pltpu.VMEM((2, 512, SPAN), BF16),
             pltpu.VMEM((2, 88 + SPAN, 512), F32),
+            pltpu.VMEM((2, 256, 2 * SPAN), F32),
             dma((8,)),
             pltpu.SemaphoreType.REGULAR,
             dma,
             dma,
-            *[dma((PARTS,)) for _ in range(6)],
+            *[dma((PARTS,)) for _ in range(4)],
+            dma((PARTS, 4)),
+            dma((PARTS,)),
             dma((30,)),
             dma,
             dma,

time: 50.4 us -> 50.2 us (level)
  no operation moved by 1% of the time
where the time goes in v5:
time: 50.2 us; the launch traced here: 49.8 us
  Pallas kernels  49.1 us (98%)
  between operations  0.64 us (1%)
    pallas_call x1, Pallas kernels, on_device(): pl.pallas_call(body, out_shape=(jax.ShapeDtypeStruct((PARTS, 64, 2, 8, SP...  45.4 us
    pallas_call x1, Pallas kernels, on_device(): pl.pallas_call(tail, out_shape=(jax.ShapeDtypeStruct((2, 2 * TIME * 2, 12...  3.69 us

profile of v5, /device:TPU:1, one launch (start us, length us, event | category | flops | bytes accessed | tf_op | source)
XLA Modules:
  0.0 49.8 jit_solution(18245185417416329653)
XLA Ops:
  0.6 45.4 %beamform.1 = (bf16[2,64,2,8,128]{4,3,2,1,0:T(8,128)(2,1)S(1)}, bf16[2,1280,512]{2,1,0:T(8,128)(2,1)S(1)}, bf16[512,512]{1,0:T(8,128)(2,1)S(1)}, f32[12,512]{1,0...) custom-call(bf16[16,4,2,2,16,256]{5,4,3,2,1,0:T(8,128)(2,1)} %bitcast.8, ...), custom_call_target="tpu_custom_call" | custom-call | tf_op jit(solution)/shard_map/beamform/pallas_call | solution.py:432
  46.1 3.7 %synthesis.1 = (bf16[2,1024,128]{2,1,0:T(8,128)(2,1)}, f32[2,256]{1,0:T(2,128)}) custom-call(bf16[2,1024,128]{2,1,0:T(8,128)(2,1)S(1)} %bitcast.7, bf16[2,1280,512]{2,1,0:T(8,128)(2,1)S(1)} %get-tuple-element.12.tv, bf16[512,512]{1,0:T(8,128)(2,1)S(1)} %get-tuple-element.13.dftv, f32[12,512]{1,0:T(8,128)S(1)} %get-tuple-element.14.protov, ...), custom_call_target="tpu_custom_call" | custom-call | tf_op jit(solution)/shard_map/synthesis/pallas_call | solution.py:487

commit v6 on v5

--- a/solution.py
+++ b/solution.py
@@ -66,7 +66,7 @@
     return jnp.dot(a, b, preferred_element_type=F32)
 
 
-def exchange_order():
+def exchange_order(far_first=False):
     left = [(dz, dy, dx) for dz in range(4) for dy in range(4) for dx in range(4)]
     random.Random(7).shuffle(left)
     hops, ordered = [0, 0, 0], []
@@ -78,7 +78,7 @@
         left.remove(best)
         ordered.append(best)
         hops = [done + min(d, 4 - d) for done, d in zip(hops, best)]
-    return ordered
+    return sorted(ordered, key=lambda step: -sum(min(d, 4 - d) for d in step)) if far_first else ordered
 
 
 def body(
@@ -114,31 +114,10 @@
     for peer in greeted:
         pl.semaphore_signal(barrier, inc=1, device_id=peer, device_id_type=MESH)
 
-    def hand_over(part, give, send, given, sibling_sem):
+    def hand_over(give, share, given, sibling_sem):
         pltpu.make_async_remote_copy(
-            src_ref=give.at[part],
-            dst_ref=send.at[part, :, :, :, core] if len(send.shape) == 8 else send.at[part, :, core],
-            send_sem=given,
-            recv_sem=sibling_sem.at[part],
-            device_id=sibling,
-            device_id_type=MESH,
+            src_ref=give, dst_ref=share, send_sem=given, recv_sem=sibling_sem, device_id=sibling, device_id_type=MESH
         ).start()
-
-    def exchange(part, send, landing, sibling_sem, sent, recv_sem):
-        share = send.at[part, :, 1 - core]
-        pltpu.make_async_copy(share, share, sibling_sem.at[part]).wait()
-        pltpu.make_async_copy(send.at[part, chip], landing, recv_sem.at[part]).start()
-        for dz, dy, dx in exchange_order():
-            if (dz, dy, dx) != (0, 0, 0):
-                chan = ys[dy] + xs[dx]
-                pltpu.make_async_remote_copy(
-                    src_ref=send.at[part, zs[dz] * CHAN_AXIS + chan],
-                    dst_ref=landing,
-                    send_sem=sent.at[part],
-                    recv_sem=recv_sem.at[part],
-                    device_id=(zs[dz] * 2 + core, chan),
-                    device_id_type=MESH,
-                ).start()
 
     by_z, by_x, by_y, by_xz, by_yz, by_xy, by_xyz = stages
 
@@ -230,7 +209,7 @@
     for peer in line:
         pl.semaphore_signal(plane_sem, inc=1, device_id=peer, device_id_type=MESH)
     for part in range(PARTS):
-        hand_over(part, give, send, given, sibling_sem)
+        hand_over(give.at[part], send.at[part, :, :, :, core], given, sibling_sem.at[part])
     volt_loads[1].wait()
     for mz, my, block in sort_out(core):
         for part in range(PARTS):
@@ -298,14 +277,31 @@
                     acc[c] += product
                 else:
                     beams[c] = (acc[c] + product).astype(BF16)
-        for zz in range(4):
-            rows = slice(zz * 64, zz * 64 + 64)
+        for dz in (0, 2, 1, 3):
+            rows = pl.ds(pl.multiple_of(zs[dz] * 64, 64), 64)
+            chips = pl.ds(pl.multiple_of(zs[dz] * 16, 16), 16)
             block = jnp.concatenate([beams[c, rows, q * SPAN : q * SPAN + SPAN] for c in range(2) for q in range(2)], axis=0)
             block = dot(order, block).astype(BF16)
-            send2[part, zz * 16 : zz * 16 + 16, core] = block[:128].reshape(16, 8, SPAN)
-            give2[part, zz * 16 : zz * 16 + 16] = block[128:].reshape(16, 8, SPAN)
-        hand_over(part, give2, send2, given2, sibling_sem2)
-        exchange(part, send2, recv2.at[part, chip], sibling_sem2, sent2, recv_sem2)
+            give2[part, chips] = block[128:].reshape(16, 8, SPAN)
+            hand_over(give2.at[part, chips], send2.at[part, chips, core], given2, sibling_sem2.at[part, -dz % 4])
+            send2[part, chips, core] = block[:128].reshape(16, 8, SPAN)
+        for dz in (0, 2, 1, 3):
+            chips = pl.ds(pl.multiple_of(zs[dz] * 16, 16), 16)
+            share = send2.at[part, chips, 1 - core]
+            pltpu.make_async_copy(share, share, sibling_sem2.at[part, dz]).wait()
+            if dz == 0:
+                pltpu.make_async_copy(send2.at[part, chip], recv2.at[part, chip], recv_sem2.at[part]).start()
+            for steps in exchange_order(far_first=True):
+                if steps[0] == dz and steps != (0, 0, 0):
+                    stn, chan = place(steps)
+                    pltpu.make_async_remote_copy(
+                        src_ref=send2.at[part, zs[dz] * CHAN_AXIS + chan],
+                        dst_ref=recv2.at[part, chip],
+                        send_sem=sent2.at[part],
+                        recv_sem=recv_sem2.at[part],
+                        device_id=(stn, chan),
+                        device_id_type=MESH,
+                    ).start()
 
     arrived = recv2.at[0]
     pltpu.make_async_copy(arrived, arrived, recv_sem2.at[0]).wait()
@@ -462,7 +458,8 @@
             pltpu.SemaphoreType.REGULAR,
             dma,
             dma,
-            *[dma((PARTS,)) for _ in range(4)],
+            *[dma((PARTS,)) for _ in range(3)],
+            dma((PARTS, 4)),
             dma((PARTS, 4)),
             dma((PARTS,)),
             dma((30,)),

time: 50.2 us -> 50.4 us (level)
  no operation moved by 1% of the time
where the time goes in v6:
time: 50.4 us; the launch traced here: 50.2 us
  Pallas kernels  49.5 us (98%)
  between operations  0.64 us (1%)
    pallas_call x1, Pallas kernels, on_device(): pl.pallas_call(body, out_shape=(jax.ShapeDtypeStruct((PARTS, 64, 2, 8, SP...  45.8 us
    pallas_call x1, Pallas kernels, on_device(): pl.pallas_call(tail, out_shape=(jax.ShapeDtypeStruct((2, 2 * TIME * 2, 12...  3.7 us

profile of v6, /device:TPU:1, one launch (start us, length us, event | category | flops | bytes accessed | tf_op | source)
XLA Modules:
  0.0 50.2 jit_solution(10015017232320030461)
XLA Ops:
  0.6 45.8 %beamform.1 = (bf16[2,64,2,8,128]{4,3,2,1,0:T(8,128)(2,1)S(1)}, bf16[2,1280,512]{2,1,0:T(8,128)(2,1)S(1)}, bf16[512,512]{1,0:T(8,128)(2,1)S(1)}, f32[12,512]{1,0...) custom-call(bf16[16,4,2,2,16,256]{5,4,3,2,1,0:T(8,128)(2,1)} %bitcast.8, ...), custom_call_target="tpu_custom_call" | custom-call | tf_op jit(solution)/shard_map/beamform/pallas_call | solution.py:428
  46.5 3.7 %synthesis.1 = (bf16[2,1024,128]{2,1,0:T(8,128)(2,1)}, f32[2,256]{1,0:T(2,128)}) custom-call(bf16[2,1024,128]{2,1,0:T(8,128)(2,1)S(1)} %bitcast.7, bf16[2,1280,512]{2,1,0:T(8,128)(2,1)S(1)} %get-tuple-element.12.tv, bf16[512,512]{1,0:T(8,128)(2,1)S(1)} %get-tuple-element.13.dftv, f32[12,512]{1,0:T(8,128)S(1)} %get-tuple-element.14.protov, ...), custom_call_target="tpu_custom_call" | custom-call | tf_op jit(solution)/shard_map/synthesis/pallas_call | solution.py:484

commit v7 on v5

--- a/solution.py
+++ b/solution.py
@@ -82,8 +82,8 @@
 
 
 def body(
-    volt, wgt, flags, dm, chirps, dft, proto, recv2, tables, dftv, protov, series0, last0, power0,
-    vin, give, send, recv, win, chv, flagv, dmv, beams, give2, send2, keep, ordered, padded, acc,
+    volt, wgt, flags, dm, chirps, dft, proto, recv2, tables, dftv, protov, product0, last0, power0,
+    vin, give, send, recv, win, chv, flagv, dmv, beams, give2, send2, keep, ordered, padded, even, odd, acc,
     load_sem, plane_sem, given, given2, sent, sent2, sibling_sem, sibling_sem2, recv_sem, recv_sem2, pack_sem, packs_sent, relays_sent, *stages,
 ):
     x = lax.rem(lax.axis_index("chan"), 4)
@@ -223,12 +223,13 @@
                     yield mz, my, sorted_block[one * 128 : one * 128 + 128].reshape(4, 4, 8, 256)
 
     volt_loads[0].wait()
-    for mz, my, block in sort_out(1 - core):
+    for n, (mz, my, block) in enumerate(sort_out(1 - core)):
+        if n == 8:
+            pl.semaphore_wait(barrier, len(greeted))
+            for peer in line:
+                pl.semaphore_signal(plane_sem, inc=1, device_id=peer, device_id_type=MESH)
         for part in range(PARTS):
             give[part, mz, my] = block[..., part * SPAN : part * SPAN + SPAN]
-    pl.semaphore_wait(barrier, len(greeted))
-    for peer in line:
-        pl.semaphore_signal(plane_sem, inc=1, device_id=peer, device_id_type=MESH)
     for part in range(PARTS):
         hand_over(part, give, send, given, sibling_sem)
     volt_loads[1].wait()
@@ -317,7 +318,8 @@
     for b in range(2):
         for n in range(4):
             lanes, series = synthesise(b, n, protov, padded)
-            series0[b, :, lanes] = series
+            store_shifted(series, lanes, even, odd)
+        product0[b] = chirped(stacked_shifts(even, odd), tables[b])
 
     for blocks, sem in ((give, given), (give2, given2)):
         pltpu.make_async_copy(blocks, blocks, sem).wait()
@@ -359,9 +361,29 @@
     return lanes, series
 
 
+def store_shifted(series, lanes, even, odd):
+    after = jnp.where(iota(0, (32, 128)) % 8 == 7, 0.0, pltpu.roll(series[:32], 31, 0))
+    even[0:SPAN, lanes] = series.astype(BF16)
+    even[SPAN : SPAN + 32, lanes] = after.astype(BF16)
+    odd[0 : SPAN + 16, lanes] = jnp.concatenate([series[8:], after[:24]], axis=0).astype(BF16)
+
+
+def stacked_shifts(even, odd):
+    shifted = [even[0:SPAN], odd[0:SPAN], even[16 : 16 + SPAN], odd[16 : 16 + SPAN], even[32 : 32 + SPAN]]
+    return [jnp.concatenate([block[:, p * 256 : p * 256 + 256] for block in shifted], axis=1) for p in range(2)]
+
+
+def chirped(parts, table):
+    product = dot(jnp.concatenate(parts, axis=0), table)
+    rows = product.shape[0] // 2
+    real = product[:rows, :256] + product[rows:, 256:]
+    imag = product[rows:, :256] - product[:rows, 256:]
+    return jnp.concatenate([real, imag], axis=1)
+
+
 def tail(
-    xv, tv, dftv, protov, series0, last0, power0, out, band,
-    xs, padded, even00, even01, even10, even11, odd00, odd01, odd10, odd11, outv, bandv, out_sem,
+    xv, tv, dftv, protov, product0, last0, power0, out, band,
+    xs, padded, even0, even1, odd0, odd1, over0, over1, outv, bandv, out_sem,
 ):
     band_copy = pltpu.make_async_copy(bandv, band, out_sem.at[2])
     for b, power, _ in front(lambda n: xv[1, n * 256 : n * 256 + 256, :], lambda b: last0[b], dftv, protov, xs, padded):
@@ -369,32 +391,23 @@
         bandv[b : b + 1, :] = power[:, :256] + power[:, 256:]
     band_copy.start()
     results = []
-    final_lane = iota(0, (32, 128)) % 8 == 7
-    for b, evens, odds in ((0, (even00, even01), (odd00, odd01)), (1, (even10, even11), (odd10, odd11))):
+    for b, (even, odd, over) in enumerate(((even0, odd0, over0), (even1, odd1, over1))):
         for n in range(4):
-            lanes, series1 = synthesise(b, n, protov, padded)
-            both = (series0[b, :, lanes], series1)
-            following = (pltpu.roll(series1[:32], 7, 0), 0.0)
-            for series, follow, even, odd in zip(both, following, evens, odds):
-                after = jnp.where(final_lane, follow, pltpu.roll(series[:32], 31, 0))
-                even[0:SPAN, lanes] = series.astype(BF16)
-                even[SPAN : SPAN + 32, lanes] = after.astype(BF16)
-                odd[0 : SPAN + 16, lanes] = jnp.concatenate([series[8:], after[:24]], axis=0).astype(BF16)
-        shifted = [
-            [even[0:SPAN], odd[0:SPAN], even[16 : 16 + SPAN], odd[16 : 16 + SPAN], even[32 : 32 + SPAN]]
-            for even, odd in zip(evens, odds)
+            lanes, series = synthesise(b, n, protov, padded)
+            store_shifted(series, lanes, even, odd)
+            over_edge = jnp.where(iota(0, (32, 128)) % 8 == 7, pltpu.roll(series[:32], 7, 0), 0.0)
+            for blk in range(NBLOCK):
+                seen = [over_edge[: 8 * blk]] if blk else []
+                unseen = [jnp.zeros((32 - 8 * blk, 128), F32)] if blk < 4 else []
+                over[blk, :, lanes] = jnp.concatenate(unseen + seen, axis=0).astype(BF16)
+        edges = [
+            jnp.concatenate([over[blk, :, p * 256 : p * 256 + 256] for blk in range(NBLOCK)], axis=1) for p in range(2)
         ]
-        lhs = jnp.concatenate(
-            [
-                jnp.concatenate([block[:, p * 256 : p * 256 + 256] for block in blocks], axis=1)
-                for p in range(2) for blocks in shifted
-            ],
-            axis=0,
+        parts = [jnp.concatenate(pair, axis=0) for pair in zip(stacked_shifts(even, odd), edges)]
+        product = chirped(parts, tv[b])
+        results.append(
+            jnp.concatenate([product0[b, :96], product0[b, 96:] + product[SPAN:], product[:SPAN]], axis=0).astype(BF16)
         )
-        product = dot(lhs, tv[b])
-        real = product[:256, :256] + product[256:, 256:]
-        imag = product[256:, :256] - product[:256, 256:]
-        results.append(jnp.concatenate([real, imag], axis=1).astype(BF16))
     row, col = iota(0), iota(1)
     final = ones_where(col == (row % 4) * 64 + ((row // 4) % 8) * 8 + row // 32)
     copies = []
@@ -429,7 +442,7 @@
     vmem = pl.BlockSpec(memory_space=pltpu.VMEM)
     dma = pltpu.SemaphoreType.DMA
     params = dict(vmem_limit_bytes=24 * 1024 * 1024)
-    beams, tables, dft, proto, series0, last0, power0 = pl.pallas_call(
+    beams, tables, dft, proto, product0, last0, power0 = pl.pallas_call(
         body,
         out_shape=(
             jax.ShapeDtypeStruct((PARTS, 64, 2, 8, SPAN), BF16),
@@ -457,6 +470,8 @@
             pltpu.VMEM((16, 256), F32),
             pltpu.VMEM((2, 512, SPAN), BF16),
             pltpu.VMEM((2, 88 + SPAN, 512), F32),
+            pltpu.VMEM((SPAN + 32, 512), BF16),
+            pltpu.VMEM((SPAN + 16, 512), BF16),
             pltpu.VMEM((2, 256, 2 * SPAN), F32),
             dma((8,)),
             pltpu.SemaphoreType.REGULAR,
@@ -495,8 +510,9 @@
         scratch_shapes=[
             pltpu.VMEM((2, 512, SPAN), BF16),
             pltpu.VMEM((2, 88 + SPAN, 512), F32),
-            *[pltpu.VMEM((SPAN + 32, 512), BF16) for _ in range(4)],
-            *[pltpu.VMEM((SPAN + 16, 512), BF16) for _ in range(4)],
+            *[pltpu.VMEM((SPAN + 32, 512), BF16) for _ in range(2)],
+            *[pltpu.VMEM((SPAN + 16, 512), BF16) for _ in range(2)],
+            *[pltpu.VMEM((NBLOCK, 32, 512), BF16) for _ in range(2)],
             pltpu.VMEM((2, 2 * TIME * 2, 128), BF16),
             pltpu.VMEM((2, CHANNELS), F32),
             dma((3,)),
@@ -508,7 +524,7 @@
         tables,
         dft,
         proto,
-        series0,
+        product0,
         last0,
         power0,
     )

time: 50.2 us -> 50.4 us (level)
    pallas_call x1, Pallas kernels: 45.4 us -> 45.9 us  [on_device(): pl.pallas_call(body, out_shape=(jax.ShapeDtypeStruct((PARTS, 64, 2, 8, SP...]
where the time goes in v7:
time: 50.4 us; the launch traced here: 49.9 us
  Pallas kernels  49.3 us (98%)
  between operations  0.64 us (1%)
    pallas_call x1, Pallas kernels, on_device(): pl.pallas_call(body, out_shape=(jax.ShapeDtypeStruct((PARTS, 64, 2, 8, SP...  45.9 us
    pallas_call x1, Pallas kernels, on_device(): pl.pallas_call(tail, out_shape=(jax.ShapeDtypeStruct((2, 2 * TIME * 2, 12...  3.33 us

profile of v7, /device:TPU:1, one launch (start us, length us, event | category | flops | bytes accessed | tf_op | source)
XLA Modules:
  0.0 49.9 jit_solution(11994806775914824)
XLA Ops:
  0.6 45.9 %beamform.1 = (bf16[2,64,2,8,128]{4,3,2,1,0:T(8,128)(2,1)S(1)}, bf16[2,1280,512]{2,1,0:T(8,128)(2,1)S(1)}, bf16[512,512]{1,0:T(8,128)(2,1)S(1)}, f32[12,512]{1,0...) custom-call(bf16[16,4,2,2,16,256]{5,4,3,2,1,0:T(8,128)(2,1)} %bitcast.8, ...), custom_call_target="tpu_custom_call" | custom-call | tf_op jit(solution)/shard_map/beamform/pallas_call | solution.py:445
  46.6 3.3 %synthesis.1 = (bf16[2,1024,128]{2,1,0:T(8,128)(2,1)}, f32[2,256]{1,0:T(2,128)}) custom-call(bf16[2,1024,128]{2,1,0:T(8,128)(2,1)S(1)} %bitcast.7, bf16[2,1280,512]{2,1,0:T(8,128)(2,1)S(1)} %get-tuple-element.12.tv, bf16[512,512]{1,0:T(8,128)(2,1)S(1)} %get-tuple-element.13.dftv, f32[12,512]{1,0:T(8,128)S(1)} %get-tuple-element.14.protov, ...), custom_call_target="tpu_custom_call" | custom-call | tf_op jit(solution)/shard_map/synthesis/pallas_call | solution.py:502

commit v8 on v7

--- a/solution.py
+++ b/solution.py
@@ -223,13 +223,12 @@
                     yield mz, my, sorted_block[one * 128 : one * 128 + 128].reshape(4, 4, 8, 256)
 
     volt_loads[0].wait()
-    for n, (mz, my, block) in enumerate(sort_out(1 - core)):
-        if n == 8:
-            pl.semaphore_wait(barrier, len(greeted))
-            for peer in line:
-                pl.semaphore_signal(plane_sem, inc=1, device_id=peer, device_id_type=MESH)
+    for mz, my, block in sort_out(1 - core):
         for part in range(PARTS):
             give[part, mz, my] = block[..., part * SPAN : part * SPAN + SPAN]
+    pl.semaphore_wait(barrier, len(greeted))
+    for peer in line:
+        pl.semaphore_signal(plane_sem, inc=1, device_id=peer, device_id_type=MESH)
     for part in range(PARTS):
         hand_over(part, give, send, given, sibling_sem)
     volt_loads[1].wait()

time: 50.4 us -> 49.9 us (0.990)
  Pallas kernels: 49.3 us -> 48.7 us
    pallas_call x1, Pallas kernels: 45.9 us -> 45.4 us  [on_device(): pl.pallas_call(body, out_shape=(jax.ShapeDtypeStruct((PARTS, 64, 2, 8, SP...]
where the time goes in v8:
time: 49.9 us; the launch traced here: 49.4 us
  Pallas kernels  48.7 us (98%)
  between operations  0.64 us (1%)
    pallas_call x1, Pallas kernels, on_device(): pl.pallas_call(body, out_shape=(jax.ShapeDtypeStruct((PARTS, 64, 2, 8, SP...  45.4 us
    pallas_call x1, Pallas kernels, on_device(): pl.pallas_call(tail, out_shape=(jax.ShapeDtypeStruct((2, 2 * TIME * 2, 12...  3.32 us

profile of v8, /device:TPU:1, one launch (start us, length us, event | category | flops | bytes accessed | tf_op | source)
XLA Modules:
  0.0 49.4 jit_solution(6208680871430289728)
XLA Ops:
  0.6 45.4 %beamform.1 = (bf16[2,64,2,8,128]{4,3,2,1,0:T(8,128)(2,1)S(1)}, bf16[2,1280,512]{2,1,0:T(8,128)(2,1)S(1)}, bf16[512,512]{1,0:T(8,128)(2,1)S(1)}, f32[12,512]{1,0...) custom-call(bf16[16,4,2,2,16,256]{5,4,3,2,1,0:T(8,128)(2,1)} %bitcast.8, ...), custom_call_target="tpu_custom_call" | custom-call | tf_op jit(solution)/shard_map/beamform/pallas_call | solution.py:444
  46.1 3.3 %synthesis.1 = (bf16[2,1024,128]{2,1,0:T(8,128)(2,1)}, f32[2,256]{1,0:T(2,128)}) custom-call(bf16[2,1024,128]{2,1,0:T(8,128)(2,1)S(1)} %bitcast.7, bf16[2,1280,512]{2,1,0:T(8,128)(2,1)S(1)} %get-tuple-element.12.tv, bf16[512,512]{1,0:T(8,128)(2,1)S(1)} %get-tuple-element.13.dftv, f32[12,512]{1,0:T(8,128)S(1)} %get-tuple-element.14.protov, ...), custom_call_target="tpu_custom_call" | custom-call | tf_op jit(solution)/shard_map/synthesis/pallas_call | solution.py:501

commit v9 on v8

--- a/solution.py
+++ b/solution.py
@@ -305,15 +305,16 @@
             send2[part, zz * 16 : zz * 16 + 16, core] = block[:128].reshape(16, 8, SPAN)
             give2[part, zz * 16 : zz * 16 + 16] = block[128:].reshape(16, 8, SPAN)
         hand_over(part, give2, send2, given2, sibling_sem2)
+        if part == 1:
+            arrived = recv2.at[0]
+            pltpu.make_async_copy(arrived, arrived, recv_sem2.at[0]).wait()
+            for b, power, last in front(
+                lambda n: recv2[0, n * 16 : n * 16 + 16].reshape(256, SPAN), lambda b: 0.0, dftv, protov, ordered, padded
+            ):
+                power0[b : b + 1, :] = power
+                last0[b] = last
         exchange(part, send2, recv2.at[part, chip], sibling_sem2, sent2, recv_sem2)
 
-    arrived = recv2.at[0]
-    pltpu.make_async_copy(arrived, arrived, recv_sem2.at[0]).wait()
-    for b, power, last in front(
-        lambda n: recv2[0, n * 16 : n * 16 + 16].reshape(256, SPAN), lambda b: 0.0, dftv, protov, ordered, padded
-    ):
-        power0[b : b + 1, :] = power
-        last0[b] = last
     for b in range(2):
         for n in range(4):
             lanes, series = synthesise(b, n, protov, padded)

time: 49.9 us -> 54.1 us (1.084)
  Pallas kernels: 48.7 us -> 53.3 us
    pallas_call x1, Pallas kernels: 45.4 us -> 50 us  [on_device(): pl.pallas_call(body, out_shape=(jax.ShapeDtypeStruct((PARTS, 64, 2, 8, SP...]
where the time goes in v9:
time: 54.1 us; the launch traced here: 54 us
  Pallas kernels  53.3 us (99%)
  between operations  0.64 us (1%)
    pallas_call x1, Pallas kernels, on_device(): pl.pallas_call(body, out_shape=(jax.ShapeDtypeStruct((PARTS, 64, 2, 8, SP...  50 us
    pallas_call x1, Pallas kernels, on_device(): pl.pallas_call(tail, out_shape=(jax.ShapeDtypeStruct((2, 2 * TIME * 2, 12...  3.34 us

profile of v9, /device:TPU:1, one launch (start us, length us, event | category | flops | bytes accessed | tf_op | source)
XLA Modules:
  0.0 54.0 jit_solution(428257544135660)
XLA Ops:
  0.6 50.0 %beamform.1 = (bf16[2,64,2,8,128]{4,3,2,1,0:T(8,128)(2,1)S(1)}, bf16[2,1280,512]{2,1,0:T(8,128)(2,1)S(1)}, bf16[512,512]{1,0:T(8,128)(2,1)S(1)}, f32[12,512]{1,0...) custom-call(bf16[16,4,2,2,16,256]{5,4,3,2,1,0:T(8,128)(2,1)} %bitcast.8, ...), custom_call_target="tpu_custom_call" | custom-call | tf_op jit(solution)/shard_map/beamform/pallas_call | solution.py:445
  50.6 3.3 %synthesis.1 = (bf16[2,1024,128]{2,1,0:T(8,128)(2,1)}, f32[2,256]{1,0:T(2,128)}) custom-call(bf16[2,1024,128]{2,1,0:T(8,128)(2,1)S(1)} %bitcast.7, bf16[2,1280,512]{2,1,0:T(8,128)(2,1)S(1)} %get-tuple-element.12.tv, bf16[512,512]{1,0:T(8,128)(2,1)S(1)} %get-tuple-element.13.dftv, f32[12,512]{1,0:T(8,128)S(1)} %get-tuple-element.14.protov, ...), custom_call_target="tpu_custom_call" | custom-call | tf_op jit(solution)/shard_map/synthesis/pallas_call | solution.py:502

commit v10 on v8

--- a/solution.py
+++ b/solution.py
@@ -246,10 +246,9 @@
     pl.semaphore_wait(plane_sem, len(line))
     send_packs(0)
     send_direct(0)
+    relay_packs(0)
     send_packs(1)
-    relay_packs(0)
     send_direct(1)
-    relay_packs(1)
     for load in loads:
         load.wait()
 
@@ -305,6 +304,8 @@
             send2[part, zz * 16 : zz * 16 + 16, core] = block[:128].reshape(16, 8, SPAN)
             give2[part, zz * 16 : zz * 16 + 16] = block[128:].reshape(16, 8, SPAN)
         hand_over(part, give2, send2, given2, sibling_sem2)
+        if part == 0:
+            relay_packs(1)
         exchange(part, send2, recv2.at[part, chip], sibling_sem2, sent2, recv_sem2)
 
     arrived = recv2.at[0]

time: 49.9 us -> 52.9 us (1.060)
  Pallas kernels: 48.7 us -> 52.1 us
    pallas_call x1, Pallas kernels: 45.4 us -> 48.8 us  [on_device(): pl.pallas_call(body, out_shape=(jax.ShapeDtypeStruct((PARTS, 64, 2, 8, SP...]
where the time goes in v10:
time: 52.9 us; the launch traced here: 52.8 us
  Pallas kernels  52.1 us (98%)
  between operations  0.64 us (1%)
    pallas_call x1, Pallas kernels, on_device(): pl.pallas_call(body, out_shape=(jax.ShapeDtypeStruct((PARTS, 64, 2, 8, SP...  48.8 us
    pallas_call x1, Pallas kernels, on_device(): pl.pallas_call(tail, out_shape=(jax.ShapeDtypeStruct((2, 2 * TIME * 2, 12...  3.33 us

profile of v10, /device:TPU:1, one launch (start us, length us, event | category | flops | bytes accessed | tf_op | source)
XLA Modules:
  0.0 52.8 jit_solution(3737508505045977811)
XLA Ops:
  0.6 48.8 %beamform.1 = (bf16[2,64,2,8,128]{4,3,2,1,0:T(8,128)(2,1)S(1)}, bf16[2,1280,512]{2,1,0:T(8,128)(2,1)S(1)}, bf16[512,512]{1,0:T(8,128)(2,1)S(1)}, f32[12,512]{1,0...) custom-call(bf16[16,4,2,2,16,256]{5,4,3,2,1,0:T(8,128)(2,1)} %bitcast.8, ...), custom_call_target="tpu_custom_call" | custom-call | tf_op jit(solution)/shard_map/beamform/pallas_call | solution.py:445
  49.5 3.3 %synthesis.1 = (bf16[2,1024,128]{2,1,0:T(8,128)(2,1)}, f32[2,256]{1,0:T(2,128)}) custom-call(bf16[2,1024,128]{2,1,0:T(8,128)(2,1)S(1)} %bitcast.7, bf16[2,1280,512]{2,1,0:T(8,128)(2,1)S(1)} %get-tuple-element.12.tv, bf16[512,512]{1,0:T(8,128)(2,1)S(1)} %get-tuple-element.13.dftv, f32[12,512]{1,0:T(8,128)S(1)} %get-tuple-element.14.protov, ...), custom_call_target="tpu_custom_call" | custom-call | tf_op jit(solution)/shard_map/synthesis/pallas_call | solution.py:502

commit v11 on v8

--- a/solution.py
+++ b/solution.py
@@ -305,6 +305,7 @@
             send2[part, zz * 16 : zz * 16 + 16, core] = block[:128].reshape(16, 8, SPAN)
             give2[part, zz * 16 : zz * 16 + 16] = block[128:].reshape(16, 8, SPAN)
         hand_over(part, give2, send2, given2, sibling_sem2)
+    for part in range(PARTS):
         exchange(part, send2, recv2.at[part, chip], sibling_sem2, sent2, recv_sem2)
 
     arrived = recv2.at[0]

time: 49.9 us -> 51.9 us (1.040)
  Pallas kernels: 48.7 us -> 51.1 us
    pallas_call x1, Pallas kernels: 45.4 us -> 47.8 us  [on_device(): pl.pallas_call(body, out_shape=(jax.ShapeDtypeStruct((PARTS, 64, 2, 8, SP...]
where the time goes in v11:
time: 51.9 us; the launch traced here: 51.8 us
  Pallas kernels  51.1 us (98%)
  between operations  0.64 us (1%)
    pallas_call x1, Pallas kernels, on_device(): pl.pallas_call(body, out_shape=(jax.ShapeDtypeStruct((PARTS, 64, 2, 8, SP...  47.8 us
    pallas_call x1, Pallas kernels, on_device(): pl.pallas_call(tail, out_shape=(jax.ShapeDtypeStruct((2, 2 * TIME * 2, 12...  3.32 us

profile of v11, /device:TPU:1, one launch (start us, length us, event | category | flops | bytes accessed | tf_op | source)
XLA Modules:
  0.0 51.8 jit_solution(9258874047765063231)
XLA Ops:
  0.6 47.8 %beamform.1 = (bf16[2,64,2,8,128]{4,3,2,1,0:T(8,128)(2,1)S(1)}, bf16[2,1280,512]{2,1,0:T(8,128)(2,1)S(1)}, bf16[512,512]{1,0:T(8,128)(2,1)S(1)}, f32[12,512]{1,0...) custom-call(bf16[16,4,2,2,16,256]{5,4,3,2,1,0:T(8,128)(2,1)} %bitcast.8, ...), custom_call_target="tpu_custom_call" | custom-call | tf_op jit(solution)/shard_map/beamform/pallas_call | solution.py:445
  48.5 3.3 %synthesis.1 = (bf16[2,1024,128]{2,1,0:T(8,128)(2,1)}, f32[2,256]{1,0:T(2,128)}) custom-call(bf16[2,1024,128]{2,1,0:T(8,128)(2,1)S(1)} %bitcast.7, bf16[2,1280,512]{2,1,0:T(8,128)(2,1)S(1)} %get-tuple-element.12.tv, bf16[512,512]{1,0:T(8,128)(2,1)S(1)} %get-tuple-element.13.dftv, f32[12,512]{1,0:T(8,128)S(1)} %get-tuple-element.14.protov, ...), custom_call_target="tpu_custom_call" | custom-call | tf_op jit(solution)/shard_map/synthesis/pallas_call | solution.py:502

commit v12 on v8

--- a/solution.py
+++ b/solution.py
@@ -264,7 +264,6 @@
                 tables[b, rows, part * CHANNELS : (part + 1) * CHANNELS] = jnp.concatenate(both, axis=0).astype(BF16)
         return carry
 
-    lax.fori_loop(0, 2 * NBLOCK, toeplitz, 0)
 
     to_device = lax.rem(core + row // 128, 2) * 16 + (row // 8) % 16
     order = ones_where(
@@ -305,6 +304,8 @@
             send2[part, zz * 16 : zz * 16 + 16, core] = block[:128].reshape(16, 8, SPAN)
             give2[part, zz * 16 : zz * 16 + 16] = block[128:].reshape(16, 8, SPAN)
         hand_over(part, give2, send2, given2, sibling_sem2)
+        if part == 0:
+            lax.fori_loop(0, 2 * NBLOCK, toeplitz, 0)
         exchange(part, send2, recv2.at[part, chip], sibling_sem2, sent2, recv_sem2)
 
     arrived = recv2.at[0]

time: 49.9 us -> 49.5 us (level)
  no operation moved by 1% of the time
where the time goes in v12:
time: 49.5 us; the launch traced here: 49.1 us
  Pallas kernels  48.5 us (98%)
  between operations  0.64 us (1%)
    pallas_call x1, Pallas kernels, on_device(): pl.pallas_call(body, out_shape=(jax.ShapeDtypeStruct((PARTS, 64, 2, 8, SP...  45.1 us
    pallas_call x1, Pallas kernels, on_device(): pl.pallas_call(tail, out_shape=(jax.ShapeDtypeStruct((2, 2 * TIME * 2, 12...  3.33 us

profile of v12, /device:TPU:1, one launch (start us, length us, event | category | flops | bytes accessed | tf_op | source)
XLA Modules:
  0.0 49.1 jit_solution(7345374006770195968)
XLA Ops:
  0.6 45.1 %beamform.1 = (bf16[2,64,2,8,128]{4,3,2,1,0:T(8,128)(2,1)S(1)}, bf16[2,1280,512]{2,1,0:T(8,128)(2,1)S(1)}, bf16[512,512]{1,0:T(8,128)(2,1)S(1)}, f32[12,512]{1,0...) custom-call(bf16[16,4,2,2,16,256]{5,4,3,2,1,0:T(8,128)(2,1)} %bitcast.8, ...), custom_call_target="tpu_custom_call" | custom-call | tf_op jit(solution)/shard_map/beamform/pallas_call | solution.py:445
  45.8 3.3 %synthesis.1 = (bf16[2,1024,128]{2,1,0:T(8,128)(2,1)}, f32[2,256]{1,0:T(2,128)}) custom-call(bf16[2,1024,128]{2,1,0:T(8,128)(2,1)S(1)} %bitcast.7, bf16[2,1280,512]{2,1,0:T(8,128)(2,1)S(1)} %get-tuple-element.12.tv, bf16[512,512]{1,0:T(8,128)(2,1)S(1)} %get-tuple-element.13.dftv, f32[12,512]{1,0:T(8,128)S(1)} %get-tuple-element.14.protov, ...), custom_call_target="tpu_custom_call" | custom-call | tf_op jit(solution)/shard_map/synthesis/pallas_call | solution.py:502

commit v13 on v12

--- a/solution.py
+++ b/solution.py
@@ -186,8 +186,8 @@
                     device_id_type=MESH,
                 ).start()
 
-    def relay_packs(part):
-        for n, _, stage, steps, onward in packs(part):
+    def relay_packs(part, some=slice(None)):
+        for n, _, stage, steps, onward in packs(part)[some]:
             pltpu.make_async_copy(stage, stage, pack_sem.at[n]).wait()
             dz, dy, dx = (-d % 4 for d in steps)
             origin = zs[dz] * CHAN_AXIS + ys[dy] + xs[dx]
@@ -249,7 +249,7 @@
     send_packs(1)
     relay_packs(0)
     send_direct(1)
-    relay_packs(1)
+    relay_packs(1, slice(0, 8))
     for load in loads:
         load.wait()
 
@@ -305,6 +305,8 @@
             give2[part, zz * 16 : zz * 16 + 16] = block[128:].reshape(16, 8, SPAN)
         hand_over(part, give2, send2, given2, sibling_sem2)
         if part == 0:
+            relay_packs(1, slice(8, None))
+        else:
             lax.fori_loop(0, 2 * NBLOCK, toeplitz, 0)
         exchange(part, send2, recv2.at[part, chip], sibling_sem2, sent2, recv_sem2)
 

time: 49.5 us -> 53.8 us (1.087)
  Pallas kernels: 48.5 us -> 53.1 us
    pallas_call x1, Pallas kernels: 45.1 us -> 49.7 us  [on_device(): pl.pallas_call(body, out_shape=(jax.ShapeDtypeStruct((PARTS, 64, 2, 8, SP...]
where the time goes in v13:
time: 53.8 us; the launch traced here: 53.7 us
  Pallas kernels  53.1 us (99%)
  between operations  0.64 us (1%)
    pallas_call x1, Pallas kernels, on_device(): pl.pallas_call(body, out_shape=(jax.ShapeDtypeStruct((PARTS, 64, 2, 8, SP...  49.7 us
    pallas_call x1, Pallas kernels, on_device(): pl.pallas_call(tail, out_shape=(jax.ShapeDtypeStruct((2, 2 * TIME * 2, 12...  3.32 us

profile of v13, /device:TPU:1, one launch (start us, length us, event | category | flops | bytes accessed | tf_op | source)
XLA Modules:
  0.0 53.7 jit_solution(11212366014429158612)
XLA Ops:
  0.6 49.7 %beamform.1 = (bf16[2,64,2,8,128]{4,3,2,1,0:T(8,128)(2,1)S(1)}, bf16[2,1280,512]{2,1,0:T(8,128)(2,1)S(1)}, bf16[512,512]{1,0:T(8,128)(2,1)S(1)}, f32[12,512]{1,0...) custom-call(bf16[16,4,2,2,16,256]{5,4,3,2,1,0:T(8,128)(2,1)} %bitcast.8, ...), custom_call_target="tpu_custom_call" | custom-call | tf_op jit(solution)/shard_map/beamform/pallas_call | solution.py:447
  50.4 3.3 %synthesis.1 = (bf16[2,1024,128]{2,1,0:T(8,128)(2,1)}, f32[2,256]{1,0:T(2,128)}) custom-call(bf16[2,1024,128]{2,1,0:T(8,128)(2,1)S(1)} %bitcast.7, bf16[2,1280,512]{2,1,0:T(8,128)(2,1)S(1)} %get-tuple-element.12.tv, bf16[512,512]{1,0:T(8,128)(2,1)S(1)} %get-tuple-element.13.dftv, f32[12,512]{1,0:T(8,128)S(1)} %get-tuple-element.14.protov, ...), custom_call_target="tpu_custom_call" | custom-call | tf_op jit(solution)/shard_map/synthesis/pallas_call | solution.py:504

commit v14 on v12

--- a/solution.py
+++ b/solution.py
@@ -245,8 +245,8 @@
         load.start()
     pl.semaphore_wait(plane_sem, len(line))
     send_packs(0)
+    send_packs(1)
     send_direct(0)
-    send_packs(1)
     relay_packs(0)
     send_direct(1)
     relay_packs(1)

time: 49.5 us -> 49.8 us (level)
  Pallas kernels: 48.5 us -> 49 us
    pallas_call x1, Pallas kernels: 45.1 us -> 45.7 us  [on_device(): pl.pallas_call(body, out_shape=(jax.ShapeDtypeStruct((PARTS, 64, 2, 8, SP...]
where the time goes in v14:
time: 49.8 us; the launch traced here: 49.7 us
  Pallas kernels  49 us (98%)
  between operations  0.64 us (1%)
    pallas_call x1, Pallas kernels, on_device(): pl.pallas_call(body, out_shape=(jax.ShapeDtypeStruct((PARTS, 64, 2, 8, SP...  45.7 us
    pallas_call x1, Pallas kernels, on_device(): pl.pallas_call(tail, out_shape=(jax.ShapeDtypeStruct((2, 2 * TIME * 2, 12...  3.34 us

profile of v14, /device:TPU:1, one launch (start us, length us, event | category | flops | bytes accessed | tf_op | source)
XLA Modules:
  0.0 49.7 jit_solution(15399153024093131316)
XLA Ops:
  0.6 45.7 %beamform.1 = (bf16[2,64,2,8,128]{4,3,2,1,0:T(8,128)(2,1)S(1)}, bf16[2,1280,512]{2,1,0:T(8,128)(2,1)S(1)}, bf16[512,512]{1,0:T(8,128)(2,1)S(1)}, f32[12,512]{1,0...) custom-call(bf16[16,4,2,2,16,256]{5,4,3,2,1,0:T(8,128)(2,1)} %bitcast.8, ...), custom_call_target="tpu_custom_call" | custom-call | tf_op jit(solution)/shard_map/beamform/pallas_call | solution.py:445
  46.3 3.3 %synthesis.1 = (bf16[2,1024,128]{2,1,0:T(8,128)(2,1)}, f32[2,256]{1,0:T(2,128)}) custom-call(bf16[2,1024,128]{2,1,0:T(8,128)(2,1)S(1)} %bitcast.7, bf16[2,1280,512]{2,1,0:T(8,128)(2,1)S(1)} %get-tuple-element.12.tv, bf16[512,512]{1,0:T(8,128)(2,1)S(1)} %get-tuple-element.13.dftv, f32[12,512]{1,0:T(8,128)S(1)} %get-tuple-element.14.protov, ...), custom_call_target="tpu_custom_call" | custom-call | tf_op jit(solution)/shard_map/synthesis/pallas_call | solution.py:502

commit v15 on v12

--- a/solution.py
+++ b/solution.py
@@ -248,8 +248,8 @@
     send_direct(0)
     send_packs(1)
     relay_packs(0)
+    relay_packs(1)
     send_direct(1)
-    relay_packs(1)
     for load in loads:
         load.wait()
 

time: 49.5 us -> 50.3 us (1.016)
  Pallas kernels: 48.5 us -> 49.5 us
    pallas_call x1, Pallas kernels: 45.1 us -> 46.2 us  [on_device(): pl.pallas_call(body, out_shape=(jax.ShapeDtypeStruct((PARTS, 64, 2, 8, SP...]
where the time goes in v15:
time: 50.3 us; the launch traced here: 50.2 us
  Pallas kernels  49.5 us (98%)
  between operations  0.64 us (1%)
    pallas_call x1, Pallas kernels, on_device(): pl.pallas_call(body, out_shape=(jax.ShapeDtypeStruct((PARTS, 64, 2, 8, SP...  46.2 us
    pallas_call x1, Pallas kernels, on_device(): pl.pallas_call(tail, out_shape=(jax.ShapeDtypeStruct((2, 2 * TIME * 2, 12...  3.34 us

profile of v15, /device:TPU:1, one launch (start us, length us, event | category | flops | bytes accessed | tf_op | source)
XLA Modules:
  0.0 50.2 jit_solution(5066783260923714368)
XLA Ops:
  0.6 46.2 %beamform.1 = (bf16[2,64,2,8,128]{4,3,2,1,0:T(8,128)(2,1)S(1)}, bf16[2,1280,512]{2,1,0:T(8,128)(2,1)S(1)}, bf16[512,512]{1,0:T(8,128)(2,1)S(1)}, f32[12,512]{1,0...) custom-call(bf16[16,4,2,2,16,256]{5,4,3,2,1,0:T(8,128)(2,1)} %bitcast.8, ...), custom_call_target="tpu_custom_call" | custom-call | tf_op jit(solution)/shard_map/beamform/pallas_call | solution.py:445
  46.8 3.3 %synthesis.1 = (bf16[2,1024,128]{2,1,0:T(8,128)(2,1)}, f32[2,256]{1,0:T(2,128)}) custom-call(bf16[2,1024,128]{2,1,0:T(8,128)(2,1)S(1)} %bitcast.7, bf16[2,1280,512]{2,1,0:T(8,128)(2,1)S(1)} %get-tuple-element.12.tv, bf16[512,512]{1,0:T(8,128)(2,1)S(1)} %get-tuple-element.13.dftv, f32[12,512]{1,0:T(8,128)S(1)} %get-tuple-element.14.protov, ...), custom_call_target="tpu_custom_call" | custom-call | tf_op jit(solution)/shard_map/synthesis/pallas_call | solution.py:502

commit v16 on v12

--- a/solution.py
+++ b/solution.py
@@ -125,8 +125,9 @@
         ).start()
 
     def exchange(part, send, landing, sibling_sem, sent, recv_sem):
-        share = send.at[part, :, 1 - core]
-        pltpu.make_async_copy(share, share, sibling_sem.at[part]).wait()
+        for zz in range(4):
+            share = send.at[part, zz * 16 : zz * 16 + 16, 1 - core]
+            pltpu.make_async_copy(share, share, sibling_sem.at[part, zz]).wait()
         pltpu.make_async_copy(send.at[part, chip], landing, recv_sem.at[part]).start()
         for dz, dy, dx in exchange_order():
             if (dz, dy, dx) != (0, 0, 0):
@@ -301,9 +302,17 @@
             rows = slice(zz * 64, zz * 64 + 64)
             block = jnp.concatenate([beams[c, rows, q * SPAN : q * SPAN + SPAN] for c in range(2) for q in range(2)], axis=0)
             block = dot(order, block).astype(BF16)
-            send2[part, zz * 16 : zz * 16 + 16, core] = block[:128].reshape(16, 8, SPAN)
-            give2[part, zz * 16 : zz * 16 + 16] = block[128:].reshape(16, 8, SPAN)
-        hand_over(part, give2, send2, given2, sibling_sem2)
+            chips = pl.ds(zz * 16, 16)
+            give2[part, chips] = block[128:].reshape(16, 8, SPAN)
+            pltpu.make_async_remote_copy(
+                src_ref=give2.at[part, chips],
+                dst_ref=send2.at[part, chips, core],
+                send_sem=given2,
+                recv_sem=sibling_sem2.at[part, zz],
+                device_id=sibling,
+                device_id_type=MESH,
+            ).start()
+            send2[part, chips, core] = block[:128].reshape(16, 8, SPAN)
         if part == 0:
             lax.fori_loop(0, 2 * NBLOCK, toeplitz, 0)
         exchange(part, send2, recv2.at[part, chip], sibling_sem2, sent2, recv_sem2)
@@ -477,7 +486,8 @@
             pltpu.SemaphoreType.REGULAR,
             dma,
             dma,
-            *[dma((PARTS,)) for _ in range(4)],
+            *[dma((PARTS,)) for _ in range(3)],
+            dma((PARTS, 4)),
             dma((PARTS, 4)),
             dma((PARTS,)),
             dma((30,)),

time: 49.5 us -> 49.9 us (level)
  Pallas kernels: 48.5 us -> 49 us
    pallas_call x1, Pallas kernels: 45.1 us -> 45.7 us  [on_device(): pl.pallas_call(body, out_shape=(jax.ShapeDtypeStruct((PARTS, 64, 2, 8, SP...]
where the time goes in v16:
time: 49.9 us; the launch traced here: 49.6 us
  Pallas kernels  49 us (98%)
  between operations  0.64 us (1%)
    pallas_call x1, Pallas kernels, on_device(): pl.pallas_call(body, out_shape=(jax.ShapeDtypeStruct((PARTS, 64, 2, 8, SP...  45.7 us
    pallas_call x1, Pallas kernels, on_device(): pl.pallas_call(tail, out_shape=(jax.ShapeDtypeStruct((2, 2 * TIME * 2, 12...  3.33 us

profile of v16, /device:TPU:1, one launch (start us, length us, event | category | flops | bytes accessed | tf_op | source)
XLA Modules:
  0.0 49.6 jit_solution(14410270347555510225)
XLA Ops:
  0.6 45.7 %beamform.1 = (bf16[2,64,2,8,128]{4,3,2,1,0:T(8,128)(2,1)S(1)}, bf16[2,1280,512]{2,1,0:T(8,128)(2,1)S(1)}, bf16[512,512]{1,0:T(8,128)(2,1)S(1)}, f32[12,512]{1,0...) custom-call(bf16[16,4,2,2,16,256]{5,4,3,2,1,0:T(8,128)(2,1)} %bitcast.8, ...), custom_call_target="tpu_custom_call" | custom-call | tf_op jit(solution)/shard_map/beamform/pallas_call | solution.py:454
  46.3 3.3 %synthesis.1 = (bf16[2,1024,128]{2,1,0:T(8,128)(2,1)}, f32[2,256]{1,0:T(2,128)}) custom-call(bf16[2,1024,128]{2,1,0:T(8,128)(2,1)S(1)} %bitcast.7, bf16[2,1280,512]{2,1,0:T(8,128)(2,1)S(1)} %get-tuple-element.12.tv, bf16[512,512]{1,0:T(8,128)(2,1)S(1)} %get-tuple-element.13.dftv, f32[12,512]{1,0:T(8,128)S(1)} %get-tuple-element.14.protov, ...), custom_call_target="tpu_custom_call" | custom-call | tf_op jit(solution)/shard_map/synthesis/pallas_call | solution.py:512
